TPU v7x, 32 devices: a whole 2x2x4 slice. The times are simulated.
32 devices in a mesh: table: 16 (over z, y, x), expert: 2 (over core).
Axes of the slice: x: 2, y: 2, z: 4, core: 2. Of those that a mesh axis runs over, the one named last changes fastest.
Arguments:
- table: bfloat16 [16, 512, 256], P('table'), may hold values from -127 to 127, as said below
- row_scale: float32 [16, 512], P('table'), may hold values from 0.3 to 3
- windows: int32 [16, 2, 256], P('table', 'expert'), may hold values from 0 to 511, as said below
- bag_idx: int32 [16, 2, 2048, 8], P('table', 'expert'), may hold values from 0 to 255
- bag_len: int32 [16, 2, 2048], P('table', 'expert'), may hold values from 1 to 8
- feat_gain: float32 [16, 256], replicated, may hold values from 0.03 to 0.3
- norm_gain: float32 [256], replicated, may hold values from 0.5 to 1.5
- expert_ids: int32 [2, 2048, 1], P('expert', 'table'), may hold values from 0 to 15; in each aligned block of 128 rows (0 to 127, 128 to 255, ..., all dimensions but the last counted through in order) at most 16 rows name the same one
- w_in: bfloat16 [16, 256, 4096], P('table', None, 'expert'), may hold values from -0.375 to 0.375
- w_out: bfloat16 [16, 4096, 256], P('table', 'expert'), may hold values from -0.09375 to 0.09375
- w_tow1: bfloat16 [3, 256, 256], replicated, may hold values from -0.375 to 0.375
- w_tow2: float32 [3, 256], replicated, may hold values from -1.5 to 1.5
- targets: float32 [2, 2048, 3], P('expert', 'table'), may hold values from 0 to 1
Outputs:
- predictions: float32 [2, 2048, 3], P('expert', 'table')
- grad_table: float32 [16, 512, 256], P('table', 'expert')
- grad_w_in: float32 [16, 256, 4096], P('table', None, 'expert')
- grad_w_out: float32 [16, 4096, 256], P('table', 'expert')
Inputs may be any that keep to these rules, and one draw needn't show every extreme that they name: `table`: every entry is an integer. Each row windows[f, g] holds 256 distinct row numbers of feature f's table. `expert_ids`: in each aligned block of 128 samples (the samples of one device) no expert is named by more than 16 samples.
All inputs are finite; a program needn't handle non-finite values.
Results may differ from a plain program's by a relative error of at most 0.02.
Values may be sent and summed in bfloat16 or wider, within the bound.
A program may use at most 128 MiB of HBM per device.

v0:
```python
import math

import jax
import jax.numpy as jnp
from jax import lax
from jax.sharding import PartitionSpec as P

code_range = 127.0


def silu_slope(values):
    sigma = jax.nn.sigmoid(values)
    return sigma * (1.0 + values * (1.0 - sigma))


def bag_counts(indices, lengths, window):
    total = indices.shape[0]
    block = math.gcd(total, 512)
    positions = jnp.arange(window, dtype=jnp.int32)
    slots = jnp.arange(indices.shape[1], dtype=jnp.int32)

    def count_block(operands):
        block_idx, block_len = operands
        live = (slots[None, :] < block_len[:, None]).astype(jnp.float32)
        hits = (block_idx[:, :, None] == positions[None, None, :]).astype(jnp.float32)
        return jnp.sum(hits * live[:, :, None], axis=1).astype(jnp.bfloat16)

    blocked = lax.map(
        count_block,
        (
            indices.reshape(total // block, block, indices.shape[1]),
            lengths.reshape(total // block, block),
        ),
    )
    return blocked.reshape(total, window)


def dispatch(buffer):
    arrived = lax.all_to_all(buffer, "table", split_axis=0, concat_axis=0, tiled=True)
    columns = lax.all_gather(arrived[None], "expert", axis=0, tiled=True)
    return columns.reshape(-1, buffer.shape[-1])


def column_sum(term_fn, local_rows):
    return lax.psum_scatter(
        term_fn(jnp.int32(0), lax.axis_size("expert") * local_rows).astype(jnp.bfloat16),
        "expert",
        scatter_dimension=0,
        tiled=True,
    ).astype(jnp.float32)


def send_back(result, experts, capacity):
    rows_back = result.astype(jnp.bfloat16).reshape(experts, capacity, result.shape[-1])
    arrived = lax.all_to_all(rows_back, "table", split_axis=0, concat_axis=0, tiled=True)
    return arrived.reshape(experts * capacity, result.shape[-1])


def local(
    table,
    row_scale,
    windows,
    bag_idx,
    bag_len,
    feat_gain,
    norm_gain,
    expert_ids,
    w_in,
    w_out,
    w_tow1,
    w_tow2,
    targets,
):
    owners = lax.axis_size("table")
    samples = expert_ids.shape[1]
    capacity = max(2, 2 * samples // owners)
    local_rows = owners * capacity
    contract_rows = (((0,), (0,)), ((), ()))
    contract_cols = (((1,), (1,)), ((), ()))
    window = windows[0, 0]
    picked = jnp.take(table[0], window, axis=0).astype(jnp.float32)
    scales = jnp.take(row_scale[0], window)
    dequant = (picked * scales[:, None] / code_range).astype(jnp.bfloat16)
    counts = bag_counts(bag_idx[0, 0], bag_len[0, 0], window.shape[0])
    pooled = jnp.dot(counts, dequant, preferred_element_type=jnp.float32).astype(jnp.bfloat16)
    features = lax.all_to_all(
        pooled.reshape(owners, samples, pooled.shape[-1]),
        "table",
        split_axis=0,
        concat_axis=0,
        tiled=True,
    )
    summed = jnp.sum(features.astype(jnp.float32) * feat_gain[:, None, :], axis=0)
    inverse = lax.rsqrt(jnp.mean(summed * summed, axis=-1, keepdims=True) + 1e-05)
    normed = (summed * inverse * norm_gain).astype(jnp.bfloat16)
    chosen = expert_ids[0, :, 0]
    member = (chosen[:, None] == jnp.arange(owners, dtype=jnp.int32)[None, :]).astype(jnp.int32)
    ranks = jnp.cumsum(member, axis=0) - member
    slot_of = jnp.sum(ranks * member, axis=1)
    target_slot = chosen * capacity + slot_of
    placing = (jnp.arange(local_rows, dtype=jnp.int32)[:, None] == target_slot[None, :]).astype(
        jnp.bfloat16
    )
    outgoing = jnp.dot(placing, normed, preferred_element_type=jnp.float32).astype(jnp.bfloat16)
    gathered = dispatch(outgoing.reshape(owners, capacity, outgoing.shape[-1]))
    weight_in = w_in[0]
    weight_out = w_out[0]
    pre_act = jnp.dot(gathered, weight_in, preferred_element_type=jnp.float32)
    hidden = jax.nn.silu(pre_act).astype(jnp.bfloat16)

    def forward_term(start, count):
        return jnp.dot(hidden, weight_out, preferred_element_type=jnp.float32)

    expert_out = send_back(column_sum(forward_term, local_rows), owners, capacity)
    mixture = lax.dot_general(
        placing, expert_out, contract_rows, preferred_element_type=jnp.float32
    )
    joined = (normed.astype(jnp.float32) + mixture).astype(jnp.bfloat16)
    tower_pre = jnp.einsum("be,kem->kbm", joined, w_tow1, preferred_element_type=jnp.float32)
    logits = jnp.sum(jax.nn.silu(tower_pre) * w_tow2[:, None, :], axis=-1)
    predicted = jnp.stack(
        [jax.nn.sigmoid(logits[0]), jax.nn.sigmoid(logits[1]), logits[2]], axis=-1
    )
    logit_grad = predicted - targets[0]
    tower_grad = (logit_grad.T[:, :, None] * w_tow2[:, None, :] * silu_slope(tower_pre)).astype(
        jnp.bfloat16
    )
    joined_grad = jnp.einsum(
        "kbm,kem->be", tower_grad, w_tow1, preferred_element_type=jnp.float32
    ).astype(jnp.bfloat16)
    back_rows = jnp.dot(placing, joined_grad, preferred_element_type=jnp.float32).astype(
        jnp.bfloat16
    )
    gathered_grad = dispatch(back_rows.reshape(owners, capacity, back_rows.shape[-1]))
    grad_hidden = lax.dot_general(
        gathered_grad, weight_out, contract_cols, preferred_element_type=jnp.float32
    )
    grad_pre = (grad_hidden * silu_slope(pre_act)).astype(jnp.bfloat16)
    grad_out = lax.dot_general(
        hidden, gathered_grad, contract_rows, preferred_element_type=jnp.float32
    )
    grad_in = lax.dot_general(gathered, grad_pre, contract_rows, preferred_element_type=jnp.float32)

    def backward_term(start, count):
        return lax.dot_general(
            grad_pre, weight_in, contract_cols, preferred_element_type=jnp.float32
        )

    input_grad = send_back(column_sum(backward_term, local_rows), owners, capacity)
    mixture_grad = lax.dot_general(
        placing, input_grad, contract_rows, preferred_element_type=jnp.float32
    )
    normed_grad = joined_grad.astype(jnp.float32) + mixture_grad
    scaled_grad = normed_grad * norm_gain
    summed_grad = inverse * (
        scaled_grad
        - summed * inverse * inverse * jnp.mean(scaled_grad * summed, axis=-1, keepdims=True)
    )
    feature_grad = (summed_grad[None, :, :] * feat_gain[:, None, :]).astype(jnp.bfloat16)
    returned = lax.all_to_all(
        feature_grad, "table", split_axis=0, concat_axis=0, tiled=True
    ).reshape(owners * samples, feature_grad.shape[-1])
    window_grad = lax.dot_general(
        counts, returned, contract_rows, preferred_element_type=jnp.float32
    )
    row_select = (jnp.arange(table.shape[1], dtype=jnp.int32)[:, None] == window[None, :]).astype(
        jnp.float32
    )
    row_grad = jnp.dot(row_select, window_grad, precision=lax.Precision.HIGHEST)
    table_grad = lax.psum_scatter(
        row_grad.astype(jnp.bfloat16), "expert", scatter_dimension=0, tiled=True
    ).astype(jnp.float32)
    return (predicted[None], table_grad[None], grad_in[None], grad_out[None])


def solution(mesh):
    in_specs = (
        P("table", None, None),
        P("table", None),
        P("table", "expert", None),
        P("table", "expert", None, None),
        P("table", "expert", None),
        P(),
        P(),
        P("expert", "table", None),
        P("table", None, "expert"),
        P("table", "expert", None),
        P(),
        P(),
        P("expert", "table", None),
    )
    out_specs = (
        P("expert", "table", None),
        P("table", "expert", None),
        P("table", None, "expert"),
        P("table", "expert", None),
    )
    return jax.shard_map(local, mesh=mesh, in_specs=in_specs, out_specs=out_specs, check_vma=False)
```

profile of v0, /device:TPU:0, one launch (start us, length us, event | category | flops | bytes accessed | tf_op | source)
XLA Modules:
  0.0 192.5 jit_solution(6194716458040958192)
XLA Ops:
  7.2 0.8 compare_select_fusion
  8.0 0.5 broadcast.159
  8.5 1.4 reduce.3
  9.9 2.0 %gather_fusion.1 = f32[256]{0:T(256)S(1)} fusion(f32[512]{0:T(512)} %bitcast.93, s32[1024]{0:T(1024)S(1)} %pad_clamp_fusion), kind=kCustom, calls=%fused_computation.1 | custom fusion | bytes 3072 | tf_op jit(solution)/shard_map/jit(_take)/gather | solution.py:82
  11.9 2.0 %gather_fusion = bf16[256,256]{1,0:T(8,128)(2,1)S(1)} fusion(bf16[512,256]{1,0:T(8,128)(2,1)} %bitcast.97, s32[1024]{0:T(1024)S(1)} %pad_clamp_fusion), kind=kCustom, calls=%fused_computation | custom fusion | bytes 263168 | tf_op jit(solution)/shard_map/jit(_take)/gather | solution.py:81
  13.8 16.1 %while.11 = (s32[]{:T(128)}, bf16[4,512,256]{2,1,0:T(8,128)(2,1)S(1)}, s32[4,512,8]{1,2,0:T(8,128)}, s32[4,512]{1,0:T(4,128)S(1)}, s32[]{:T(128)}) while((s32[]{:T(128)}, bf16[4,512,256]{2,1,0:T(8,128)(2,1)S(1)}, s32[4,512,8]{1,2,0:T(8,128)}, s32[4,512]{1,0:T(4,128)S(1)}, s32[]{:T(128)}) %tuple.46), condition=%wide.region_2.3_spmd.clone, body=%wide.region_0.0_spmd.clone.sunk | while | flops 3022850 | bytes 940113 | solution.py:28
  13.9 0.7 dynamic-slice_bitcast_fusion.2
  14.7 0.1 copy.31
  14.9 3.0 %select_reduce_fusion.3 = bf16[512,256]{1,0:T(8,128)(2,1)S(1)} fusion(f32[512,8]{1,0:T(8,128)S(1)} %copy.31, s32[512,8]{1,0:T(8,128)S(1)} %copy.32), kind=kLoop, calls=%fused_computation.5.clone.1 | loop fusion | flops 3014656 | bytes 294912 | tf_op jit(solution)/shard_map/while/body/eval_jaxpr/reduce_sum | solution.py:26
  17.9 0.7 dynamic-slice_bitcast_fusion.2
  18.9 3.0 %select_reduce_fusion.3 = bf16[512,256]{1,0:T(8,128)(2,1)S(1)} fusion(f32[512,8]{1,0:T(8,128)S(1)} %copy.31, s32[512,8]{1,0:T(8,128)S(1)} %copy.32), kind=kLoop, calls=%fused_computation.5.clone.1 | loop fusion | flops 3014656 | bytes 294912 | tf_op jit(solution)/shard_map/while/body/eval_jaxpr/reduce_sum | solution.py:26
  21.9 0.7 dynamic-slice_bitcast_fusion.2
  22.9 3.0 %select_reduce_fusion.3 = bf16[512,256]{1,0:T(8,128)(2,1)S(1)} fusion(f32[512,8]{1,0:T(8,128)S(1)} %copy.31, s32[512,8]{1,0:T(8,128)S(1)} %copy.32), kind=kLoop, calls=%fused_computation.5.clone.1 | loop fusion | flops 3014656 | bytes 294912 | tf_op jit(solution)/shard_map/while/body/eval_jaxpr/reduce_sum | solution.py:26
  25.9 0.7 dynamic-slice_bitcast_fusion.2
  26.9 3.0 %select_reduce_fusion.3 = bf16[512,256]{1,0:T(8,128)(2,1)S(1)} fusion(f32[512,8]{1,0:T(8,128)S(1)} %copy.31, s32[512,8]{1,0:T(8,128)S(1)} %copy.32), kind=kLoop, calls=%fused_computation.5.clone.1 | loop fusion | flops 3014656 | bytes 294912 | tf_op jit(solution)/shard_map/while/body/eval_jaxpr/reduce_sum | solution.py:26
  30.0 1.5 convolution_convert_fusion
  31.5 8.4 %all-to-all-start = ((bf16[16,128,256]{2,1,0:T(8,128)(2,1)}), bf16[16,128,256]{2,1,0:T(8,128)(2,1)S(1)}, u32[]{:S(2)}, u32[]{:S(2)}) async-start(bf16[16,128,256]{2,1,0:T(8,128)(2,1)} %bitcast.7), calls=%async_computation | async-start | bytes 2097152 | tf_op jit(solution)/shard_map/all_to_all | solution.py:86
  40.1 0.2 reduce_window_sum.11
  40.3 0.2 select_reduce_fusion.1
  40.5 23.9 %all-to-all-done = bf16[16,128,256]{2,1,0:T(8,128)(2,1)S(1)} async-done(((bf16[16,128,256]{2,1,0:T(8,128)(2,1)}), bf16[16,128,256]{2,1,0:T(8,128)(2,1)S(1)}, u32[]{:S(2)}, u32[]{:S(2)}) %all-to-all-start) | async-done | bytes 1048608 | tf_op jit(solution)/shard_map/all_to_all | solution.py:86
  64.4 0.2 multiply_reduce_fusion
  64.8 0.2 convolution_convert_fusion.5
  65.0 13.4 %all_to_all.30 = bf16[16,16,256]{2,1,0:T(8,128)(2,1)S(1)} all-to-all(bf16[16,16,256]{2,1,0:T(8,128)(2,1)S(1)} %bitcast.101), channel_id=1, replica_groups=mesh['table'=16,'expert'=2] {'table'}, dimensions={0} | all-to-all | bytes 262144 | tf_op jit(solution)/shard_map/all_to_all | solution.py:39
  78.4 2.0 %all-gather = bf16[32,16,256]{2,1,0:T(8,128)(2,1)S(1)} all-gather(bf16[16,16,256]{2,1,0:T(8,128)(2,1)S(1)} %all_to_all.30), channel_id=2, replica_groups=mesh['table'=16,'expert'=2] {'expert'}, dimensions={0}, use_global_device_ids=true | all-gather | bytes 393216 | tf_op jit(solution)/shard_map/all_gather | solution.py:40
  80.4 3.2 %multiply_convert_fusion.1 = (bf16[512,2048]{1,0:T(8,128)(2,1)S(1)}, f32[512,2048]{1,0:T(8,128)}) fusion(bf16[512,256]{1,0:T(8,128)(2,1)S(1)} %bitcast.98, bf16[1,256,2048]{2,1,0:T(8,128)(2,1)S(1)} %copy-done), kind=kOutput, calls=%fused_computation.12 | convolution fusion | flops 542113792 | bytes 7602176 | tf_op jit(solution)/shard_map/dot_general | solution.py:108
  83.6 1.3 copy-done.15
  84.9 1.4 convolution_convert_fusion.3
  86.4 5.0 %reduce-scatter.4.cloned.1.call-done = bf16[256,256]{1,0:T(8,128)(2,1)} async-done(((bf16[512,256]{1,0:T(8,128)(2,1)}), bf16[256,256]{1,0:T(8,128)(2,1)}) %reduce-scatter.4.cloned.1.call-update) | async-done | bytes 131088 | tf_op jit(solution)/shard_map/reduce_scatter | solution.py:45
  91.4 14.7 %all_to_all.31 = bf16[16,16,256]{2,1,0:T(8,128)(2,1)S(1)} all-to-all(bf16[16,16,256]{2,1,0:T(8,128)(2,1)} %bitcast.106), channel_id=1, replica_groups=mesh['table'=16,'expert'=2] {'table'}, dimensions={0} | all-to-all | bytes 262144 | tf_op jit(solution)/shard_map/all_to_all | solution.py:55
  106.1 0.5 multiply_reduce_fusion.1
  106.7 0.3 fusion.6
  107.0 0.2 convolution_convert_fusion.4
  107.2 10.8 %all_to_all.32 = bf16[16,16,256]{2,1,0:T(8,128)(2,1)S(1)} all-to-all(bf16[16,16,256]{2,1,0:T(8,128)(2,1)S(1)} %bitcast.102), channel_id=1, replica_groups=mesh['table'=16,'expert'=2] {'table'}, dimensions={0} | all-to-all | bytes 262144 | tf_op jit(solution)/shard_map/all_to_all | solution.py:39
  118.0 2.0 %all-gather.1 = bf16[32,16,256]{2,1,0:T(8,128)(2,1)S(1)} all-gather(bf16[16,16,256]{2,1,0:T(8,128)(2,1)S(1)} %all_to_all.32), channel_id=3, replica_groups=mesh['table'=16,'expert'=2] {'expert'}, dimensions={0}, use_global_device_ids=true | all-gather | bytes 393216 | tf_op jit(solution)/shard_map/all_gather | solution.py:40
  119.9 3.9 %multiply_convert_fusion = bf16[512,2048]{1,0:T(8,128)(2,1)S(1)} fusion(f32[512,2048]{1,0:T(8,128)} %get-tuple-element.84, bf16[512,256]{1,0:T(8,128)(2,1)S(1)} %bitcast.103, bf16[1,2048,256]{2,1,0:T(8,128)(2,1)S(1)} %copy-done.12), kind=kOutput, calls=%fused_computation.11 | convolution fusion | flops 546308096 | bytes 7602176 | tf_op jit(solution)/shard_map/dot_general | solution.py:135
  123.9 1.3 copy-done.1
  125.2 1.5 convolution_convert_fusion.2
  126.8 5.0 %reduce-scatter.6.cloned.1.call-done = bf16[256,256]{1,0:T(8,128)(2,1)} async-done(((bf16[512,256]{1,0:T(8,128)(2,1)}), bf16[256,256]{1,0:T(8,128)(2,1)}) %reduce-scatter.6.cloned.1.call-update) | async-done | bytes 131088 | tf_op jit(solution)/shard_map/reduce_scatter | solution.py:45
  131.8 14.7 %all_to_all.33 = bf16[16,16,256]{2,1,0:T(8,128)(2,1)S(1)} all-to-all(bf16[16,16,256]{2,1,0:T(8,128)(2,1)} %bitcast.107), channel_id=1, replica_groups=mesh['table'=16,'expert'=2] {'table'}, dimensions={0} | all-to-all | bytes 262144 | tf_op jit(solution)/shard_map/all_to_all | solution.py:55
  146.4 0.3 multiply_reduce_fusion.2
  146.9 0.2 multiply_convert_fusion.2
  147.1 29.2 %all_to_all.34 = bf16[16,128,256]{2,1,0:T(8,128)(2,1)S(1)} all-to-all(bf16[16,128,256]{2,1,0:T(8,128)(2,1)S(1)} %multiply_convert_fusion.2), channel_id=1, replica_groups=mesh['table'=16,'expert'=2] {'table'}, dimensions={0} | all-to-all | bytes 2097152 | tf_op jit(solution)/shard_map/all_to_all | solution.py:160
  176.3 0.5 fusion.35
  176.8 1.1 convolution_convert_fusion.1
  177.9 0.6 copy.26
  178.5 3.8 %convolution_bitcast_fusion.1 = f32[1,256,2048]{2,1,0:T(8,128)} fusion(bf16[512,256]{1,0:T(8,128)(2,1)S(1)} %bitcast.99, bf16[512,2048]{1,0:T(8,128)(2,1)} %copy-done.1), kind=kOutput, calls=%fused_computation.15 | convolution fusion | flops 536870912 | bytes 4456448 | tf_op jit(solution)/shard_map/dot_general | solution.py:142
  182.3 2.1 %convolution_bitcast_fusion = f32[1,2048,256]{2,1,0:T(8,128)} fusion(bf16[512,2048]{1,0:T(8,128)(2,1)S(1)} %copy-done.16, bf16[512,256]{1,0:T(8,128)(2,1)S(1)} %bitcast.104), kind=kOutput, calls=%fused_computation.14 | convolution fusion | flops 536870912 | bytes 4456448 | tf_op jit(solution)/shard_map/dot_general | solution.py:139
  184.4 1.6 bitcast_convert_fusion
  (70 shorter events, 1.6 us)
Async XLA Ops:
  7.2 73.3 %copy-start = (bf16[1,256,2048]{2,1,0:T(8,128)(2,1)S(1)}, bf16[1,256,2048]{2,1,0:T(8,128)(2,1)}, u32[]{:S(2)}) copy-start(bf16[1,256,2048]{2,1,0:T(8,128)(2,1)} %param.23) | copy-start | bytes 3145732
  13.8 16.1 %copy-start.3 = (s32[1,1,256]{2,1,0:T(1,128)S(1)}, s32[1,1,256]{2,1,0:T(1,128)}, u32[]{:S(2)}) copy-start(s32[1,1,256]{2,1,0:T(1,128)} %param.17) | copy-start | bytes 3076
  30.0 10.0 %copy-start.9 = (s32[1,128,1]{1,2,0:T(1,128)S(1)}, s32[1,128,1]{1,2,0:T(1,128)}, u32[]{:S(2)}) copy-start(s32[1,128,1]{1,2,0:T(1,128)} %param.22) | copy-start | bytes 1540
  30.0 34.4 %copy-start.2 = (f32[16,256]{1,0:T(8,128)S(1)}, f32[16,256]{1,0:T(8,128)}, u32[]{:S(2)}) copy-start(f32[16,256]{1,0:T(8,128)} %param.20) | copy-start | bytes 49156
  31.5 33.2 %copy-start.7 = (f32[256]{0:T(256)S(1)}, f32[256]{0:T(256)}, u32[]{:S(2)}) copy-start(f32[256]{0:T(256)} %param.21) | copy-start | bytes 3076
  31.5 32.9 %all-to-all-start = ((bf16[16,128,256]{2,1,0:T(8,128)(2,1)}), bf16[16,128,256]{2,1,0:T(8,128)(2,1)S(1)}, u32[]{:S(2)}, u32[]{:S(2)}) async-start(bf16[16,128,256]{2,1,0:T(8,128)(2,1)} %bitcast.7), calls=%async_computation | async-start | bytes 2097152 | tf_op jit(solution)/shard_map/all_to_all | solution.py:86
  40.0 51.4 %reduce-scatter.4.cloned.1.call-start = ((), (), s32[]{:S(2)}) async-start(), calls=%async_computation.9 | async-start | bytes 393216 | tf_op jit(solution)/shard_map/reduce_scatter | solution.py:45
  40.5 24.5 %copy-start.5 = (s32[128]{0:T(128)}, s32[128]{0:T(128)S(1)}, u32[]{:S(2)}) copy-start(s32[128]{0:T(128)S(1)} %multiply_add_fusion) | copy-start | bytes 1540
  80.4 4.5 %copy-start.11 = (bf16[1,2048,256]{2,1,0:T(8,128)(2,1)S(1)}, bf16[1,2048,256]{2,1,0:T(8,128)(2,1)}, u32[]{:S(2)}) copy-start(bf16[1,2048,256]{2,1,0:T(8,128)(2,1)} %param.24) | copy-start | bytes 3145732
  83.6 1.3 copy-start.15
  84.9 21.2 %copy-start.6 = (s32[128]{0:T(128)S(1)}, s32[128]{0:T(128)}, u32[]{:S(2)}) copy-start(s32[128]{0:T(128)} %copy-done.5) | copy-start | bytes 1540
  84.9 21.2 %copy-start.8 = (f32[256]{0:T(256)S(1)}, f32[256]{0:T(256)}, u32[]{:S(2)}) copy-start(f32[256]{0:T(256)} %param.21) | copy-start | bytes 3076
  84.9 21.2 %copy-start.13 = (bf16[3,256,256]{2,1,0:T(8,128)(2,1)S(1)}, bf16[3,256,256]{2,1,0:T(8,128)(2,1)}, u32[]{:S(2)}) copy-start(bf16[3,256,256]{2,1,0:T(8,128)(2,1)} %param.25) | copy-start | bytes 1179652
  84.9 21.2 %copy-start.14 = (f32[3,256]{1,0:T(4,128)S(1)}, f32[3,256]{1,0:T(4,128)}, u32[]{:S(2)}) copy-start(f32[3,256]{1,0:T(4,128)} %param.26) | copy-start | bytes 9220
  86.4 20.3 %copy-start.10 = (f32[1,128,3]{1,0,2:T(1,128)S(1)}, f32[1,128,3]{1,0,2:T(1,128)}, u32[]{:S(2)}) copy-start(f32[1,128,3]{1,0,2:T(1,128)} %param.27) | copy-start | bytes 4612
  86.4 45.4 %reduce-scatter.6.cloned.1.call-start = ((), (), s32[]{:S(2)}) async-start(), calls=%async_computation.10 | async-start | bytes 393216 | tf_op jit(solution)/shard_map/reduce_scatter | solution.py:45
  106.6 13.3 %copy-start.12 = (bf16[1,2048,256]{2,1,0:T(8,128)(2,1)S(1)}, bf16[1,2048,256]{2,1,0:T(8,128)(2,1)}, u32[]{:S(2)}) copy-start(bf16[1,2048,256]{2,1,0:T(8,128)(2,1)} %param.24) | copy-start | bytes 3145732
  123.9 1.3 copy-start.1
  126.7 57.6 %reduce-scatter.8.cloned.1.call-start = ((), (), s32[]{:S(2)}) async-start(), calls=%async_computation.11 | async-start | bytes 393216 | tf_op jit(solution)/shard_map/reduce_scatter | solution.py:170
  147.1 29.7 %copy-start.4 = (s32[1,1,256]{2,1,0:T(1,128)S(1)}, s32[1,1,256]{2,1,0:T(1,128)}, u32[]{:S(2)}) copy-start(s32[1,1,256]{2,1,0:T(1,128)} %param.17) | copy-start | bytes 3076
  178.5 3.8 %copy-start.16 = (bf16[512,2048]{1,0:T(8,128)(2,1)S(1)}, bf16[512,2048]{1,0:T(8,128)(2,1)}, u32[]{:S(2)}) copy-start(bf16[512,2048]{1,0:T(8,128)(2,1)} %copy-done.15) | copy-start | bytes 6291460
Sparse Core Ops, SparseCore 0:
  86.5 4.8 reduce-scatter.3
  126.8 4.8 reduce-scatter.5
  178.1 5.9 reduce-scatter.7
where the time goes:
time: 193 us
  blocking collectives  86.7 us (45%)
  waiting for transfers between devices  33.9 us (18%)
  matrix products  20.5 us (11%)
  other arithmetic  16.7 us (9%)
  between operations  14 us (7%)
  local copies, waits for them, and re-layouts  11.8 us (6%)
  starting transfers between devices  8.57 us (4%)
    all_to_all x2, blocking collectives, send_back(): lax.all_to_all(rows_back, 'table', split_axis=0, concat_axis=0, tiled=True)  29.4 us
    all_to_all x1, blocking collectives, local(): lax.all_to_all(feature_grad, 'table', split_axis=0, concat_axis=0, tiled=...  29.2 us
    all_to_all x2, blocking collectives, dispatch(): lax.all_to_all(buffer, 'table', split_axis=0, concat_axis=0, tiled=True)  24.2 us
    all_to_all x1, waiting for transfers between devices, local(): lax.all_to_all(pooled.reshape(owners, samples, pooled.shape[-1]), 'table'...  23.9 us
    reduce_sum x4, other arithmetic, count_block(): return jnp.sum(hits * live[:, :, None], axis=1).astype(jnp.bfloat16)  11.8 us
    reduce_scatter x2, waiting for transfers between devices, column_sum(): lax.psum_scatter(term_fn(jnp.int32(0), lax.axis_size('expert') * local_ro...  9.96 us
    all_to_all x1, starting transfers between devices, local(): lax.all_to_all(pooled.reshape(owners, samples, pooled.shape[-1]), 'table'...  8.45 us
    all_gather x2, blocking collectives, dispatch(): columns = lax.all_gather(arrived[None], 'expert', axis=0, tiled=True)  3.96 us
  transfers between devices with their start and end apart: 4, of which 3 were waited for; matrix products, arithmetic and copies ran while one was open for 4% of the time, Pallas kernels for 0%

commit v1 on v0

v1 whole, which is shorter than its diff:
```python
import functools

import jax
import jax.numpy as jnp
from jax import lax
from jax.experimental import pallas as pl
from jax.experimental.pallas import tpu as pltpu
from jax.sharding import PartitionSpec as P

code_range = 127.0


def silu_slope(values):
    sigma = jax.nn.sigmoid(values)
    return sigma * (1.0 + values * (1.0 - sigma))


def bag_counts(indices, lengths, window):
    slots = jnp.arange(indices.shape[1], dtype=jnp.int32)
    live = jnp.where(slots[:, None] < lengths[None, :], indices.T, -1)
    positions = jnp.arange(window, dtype=jnp.int32)
    hits = (live[:, None, :] == positions[None, :, None]).astype(jnp.float32)
    return jnp.sum(hits, axis=0).astype(jnp.bfloat16)


def exchange_kernel(owners, columns, shared, x_ref, o_ref, send_sem, recv_sem, own_sem):
    devices = owners * columns
    mine = lax.axis_index("expert") * owners + lax.axis_index("table")
    barrier = pltpu.get_barrier_semaphore()

    def place(step):
        other = lax.rem(mine + step, devices)
        return other, lax.rem(other, owners), lax.div(other, owners)

    def greet(step, carry):
        _, row, column = place(step)
        pl.semaphore_signal(
            barrier, inc=1, device_id=(row, column), device_id_type=pl.DeviceIdType.MESH
        )
        return carry

    def copy(step):
        other, row, column = place(step)
        return pltpu.make_async_remote_copy(
            src_ref=x_ref.at[row if shared else other],
            dst_ref=o_ref.at[mine],
            send_sem=send_sem.at[step],
            recv_sem=recv_sem.at[step],
            device_id=(row, column),
            device_id_type=pl.DeviceIdType.MESH,
        )

    def send(step, carry):
        copy(step).start()
        return carry

    def settle(step, carry):
        copy(step).wait()
        return carry

    lax.fori_loop(1, devices, greet, 0)
    own = pltpu.make_async_copy(
        x_ref.at[lax.axis_index("table") if shared else mine], o_ref.at[mine], own_sem
    )
    own.start()
    pl.semaphore_wait(barrier, devices - 1)
    lax.fori_loop(1, devices, send, 0)
    own.wait()
    lax.fori_loop(1, devices, settle, 0)


def exchange(blocks, shared, collective_id):
    owners, columns = lax.axis_size("table"), lax.axis_size("expert")
    devices = owners * columns
    return pl.pallas_call(
        functools.partial(exchange_kernel, owners, columns, shared),
        out_shape=jax.ShapeDtypeStruct((devices,) + blocks.shape[1:], blocks.dtype),
        in_specs=[pl.BlockSpec(memory_space=pltpu.VMEM)],
        out_specs=pl.BlockSpec(memory_space=pltpu.VMEM),
        scratch_shapes=[
            pltpu.SemaphoreType.DMA((devices,)),
            pltpu.SemaphoreType.DMA((devices,)),
            pltpu.SemaphoreType.DMA,
        ],
        compiler_params=pltpu.CompilerParams(collective_id=collective_id, has_side_effects=True),
    )(blocks)


def direct():
    return lax.axis_size("expert") == 2


def dispatch(buffer, collective_id):
    if direct():
        return exchange(buffer, True, collective_id).reshape(-1, buffer.shape[-1])
    arrived = lax.all_to_all(buffer, "table", split_axis=0, concat_axis=0, tiled=True)
    columns = lax.all_gather(arrived[None], "expert", axis=0, tiled=True)
    return columns.reshape(-1, buffer.shape[-1])


def send_back(partial, experts, capacity, collective_id):
    width = partial.shape[-1]
    partial = partial.astype(jnp.bfloat16)
    if direct():
        arrived = exchange(partial.reshape(-1, capacity, width), False, collective_id)
        arrived = arrived.reshape(2, experts * capacity, width).astype(jnp.float32)
        return (arrived[0] + arrived[1]).astype(jnp.bfloat16)
    summed = lax.psum_scatter(partial, "expert", scatter_dimension=0, tiled=True)
    arrived = lax.all_to_all(
        summed.reshape(experts, capacity, width), "table", split_axis=0, concat_axis=0, tiled=True
    )
    return arrived.reshape(experts * capacity, width)


def sum_rows(row_grad):
    row_grad = row_grad.astype(jnp.bfloat16)
    if direct():
        half = row_grad.shape[0] // 2
        column = lax.axis_index("expert")
        theirs = lax.dynamic_slice_in_dim(row_grad, (1 - column) * half, half, 0)
        ours = lax.dynamic_slice_in_dim(row_grad, column * half, half, 0)
        arrived = lax.ppermute(theirs, "expert", [(0, 1), (1, 0)])
        return ours.astype(jnp.float32) + arrived.astype(jnp.float32)
    return lax.psum_scatter(row_grad, "expert", scatter_dimension=0, tiled=True).astype(jnp.float32)


def local(
    table,
    row_scale,
    windows,
    bag_idx,
    bag_len,
    feat_gain,
    norm_gain,
    expert_ids,
    w_in,
    w_out,
    w_tow1,
    w_tow2,
    targets,
):
    owners = lax.axis_size("table")
    samples = expert_ids.shape[1]
    capacity = max(2, 2 * samples // owners)
    local_rows = owners * capacity
    contract_rows = (((0,), (0,)), ((), ()))
    contract_cols = (((1,), (1,)), ((), ()))
    window = windows[0, 0]
    row_select = (
        jnp.arange(table.shape[1], dtype=jnp.int32)[:, None] == window[None, :]
    ).astype(jnp.bfloat16)
    rows = (table[0].astype(jnp.float32) * row_scale[0][:, None] / code_range).astype(jnp.bfloat16)
    dequant = lax.dot_general(
        row_select, rows, contract_rows, preferred_element_type=jnp.float32
    ).astype(jnp.bfloat16)
    counts = bag_counts(bag_idx[0, 0], bag_len[0, 0], window.shape[0])
    pooled = lax.dot_general(counts, dequant, contract_rows, preferred_element_type=jnp.float32)
    own_gain = lax.dynamic_slice_in_dim(feat_gain, lax.axis_index("table"), 1, 0)
    weighted = (pooled.astype(jnp.bfloat16).astype(jnp.float32) * own_gain).astype(jnp.bfloat16)
    summed = lax.psum_scatter(weighted, "table", scatter_dimension=0, tiled=True).astype(
        jnp.float32
    )
    inverse = lax.rsqrt(jnp.mean(summed * summed, axis=-1, keepdims=True) + 1e-05)
    normed = (summed * inverse * norm_gain).astype(jnp.bfloat16)
    chosen = expert_ids[0, :, 0]
    member = (chosen[:, None] == jnp.arange(owners, dtype=jnp.int32)[None, :]).astype(jnp.bfloat16)
    order = jnp.arange(samples, dtype=jnp.int32)
    earlier = (order[None, :] < order[:, None]).astype(jnp.bfloat16)
    ranks = jnp.dot(earlier, member, preferred_element_type=jnp.float32)
    slot_of = jnp.sum(ranks * member.astype(jnp.float32), axis=1).astype(jnp.int32)
    target_slot = chosen * capacity + slot_of
    placing = (jnp.arange(local_rows, dtype=jnp.int32)[:, None] == target_slot[None, :]).astype(
        jnp.bfloat16
    )
    outgoing = jnp.dot(placing, normed, preferred_element_type=jnp.float32).astype(jnp.bfloat16)
    gathered = dispatch(outgoing.reshape(owners, capacity, outgoing.shape[-1]), 1)
    weight_in = w_in[0]
    weight_out = w_out[0]
    pre_act = jnp.dot(gathered, weight_in, preferred_element_type=jnp.float32)
    hidden = jax.nn.silu(pre_act).astype(jnp.bfloat16)

    forward = jnp.dot(hidden, weight_out, preferred_element_type=jnp.float32)
    expert_out = send_back(forward, owners, capacity, 2)
    mixture = lax.dot_general(
        placing, expert_out, contract_rows, preferred_element_type=jnp.float32
    )
    joined = (normed.astype(jnp.float32) + mixture).astype(jnp.bfloat16)
    tower_pre = jnp.einsum("be,kem->kbm", joined, w_tow1, preferred_element_type=jnp.float32)
    logits = jnp.sum(jax.nn.silu(tower_pre) * w_tow2[:, None, :], axis=-1)
    predicted = jnp.stack(
        [jax.nn.sigmoid(logits[0]), jax.nn.sigmoid(logits[1]), logits[2]], axis=-1
    )
    logit_grad = predicted - targets[0]
    tower_grad = (logit_grad.T[:, :, None] * w_tow2[:, None, :] * silu_slope(tower_pre)).astype(
        jnp.bfloat16
    )
    joined_grad = jnp.einsum(
        "kbm,kem->be", tower_grad, w_tow1, preferred_element_type=jnp.float32
    ).astype(jnp.bfloat16)
    back_rows = jnp.dot(placing, joined_grad, preferred_element_type=jnp.float32).astype(
        jnp.bfloat16
    )
    gathered_grad = dispatch(back_rows.reshape(owners, capacity, back_rows.shape[-1]), 3)
    grad_hidden = lax.dot_general(
        gathered_grad, weight_out, contract_cols, preferred_element_type=jnp.float32
    )
    grad_pre = (grad_hidden * silu_slope(pre_act)).astype(jnp.bfloat16)
    grad_out = lax.dot_general(
        hidden, gathered_grad, contract_rows, preferred_element_type=jnp.float32
    )
    grad_in = lax.dot_general(gathered, grad_pre, contract_rows, preferred_element_type=jnp.float32)

    backward = lax.dot_general(
        grad_pre, weight_in, contract_cols, preferred_element_type=jnp.float32
    )
    input_grad = send_back(backward, owners, capacity, 4)
    mixture_grad = lax.dot_general(
        placing, input_grad, contract_rows, preferred_element_type=jnp.float32
    )
    normed_grad = joined_grad.astype(jnp.float32) + mixture_grad
    scaled_grad = normed_grad * norm_gain
    summed_grad = inverse * (
        scaled_grad
        - summed * inverse * inverse * jnp.mean(scaled_grad * summed, axis=-1, keepdims=True)
    )
    returned = lax.all_gather(summed_grad.astype(jnp.bfloat16), "table", axis=0, tiled=True)
    window_grad = jnp.dot(counts, returned, preferred_element_type=jnp.float32) * own_gain
    row_grad = jnp.dot(
        row_select, window_grad.astype(jnp.bfloat16), preferred_element_type=jnp.float32
    )
    table_grad = sum_rows(row_grad)
    return (predicted[None], table_grad[None], grad_in[None], grad_out[None])


def solution(mesh):
    in_specs = (
        P("table", None, None),
        P("table", None),
        P("table", "expert", None),
        P("table", "expert", None, None),
        P("table", "expert", None),
        P(),
        P(),
        P("expert", "table", None),
        P("table", None, "expert"),
        P("table", "expert", None),
        P(),
        P(),
        P("expert", "table", None),
    )
    out_specs = (
        P("expert", "table", None),
        P("table", "expert", None),
        P("table", None, "expert"),
        P("table", "expert", None),
    )
    return jax.shard_map(local, mesh=mesh, in_specs=in_specs, out_specs=out_specs, check_vma=False)
```

time: 193 us -> 233 us (1.21)
  waiting for transfers between devices: 33.9 us -> 130 us
  blocking collectives: 86.7 us -> 0 us
  Pallas kernels: 0 us -> 51.4 us
  local copies, waits for them, and re-layouts: 11.8 us -> 2.37 us
  other arithmetic: 16.7 us -> 7.56 us
  starting transfers between devices: 8.57 us -> 0.15 us
  matrix products: 20.5 us -> 26.8 us
    all_to_all x5 -> x0, blocking collectives: 82.7 us -> none  [the longest x2 29.4 us: send_back(): lax.all_to_all(rows_back, 'table', split_axis=0, concat_axis=0, tiled=True)]
    reduce_scatter x3 -> x1, waiting for transfers between devices: 9.96 us -> 80.3 us  [local(): lax.psum_scatter(weighted, 'table', scatter_dimension=0, tiled=True)]
    pallas_call x0 -> x4, Pallas kernels: none -> 51.4 us  [exchange(): pl.pallas_call(functools.partial(exchange_kernel, owners, columns, shared...]
    all_gather x0 -> x1, waiting for transfers between devices: none -> 49.9 us  [local(): lax.all_gather(summed_grad.astype(jnp.bfloat16), 'table', axis=0, tiled=T...]
    all_to_all x1 -> x0, waiting for transfers between devices: 23.9 us -> none  [local(): lax.all_to_all(pooled.reshape(owners, samples, pooled.shape[-1]), 'table'...]
    reduce_sum x6 -> x1, other arithmetic: 12.2 us -> 2.11 us  [bag_counts(): return jnp.sum(hits, axis=0).astype(jnp.bfloat16)]
    all_to_all x1 -> x0, starting transfers between devices: 8.45 us -> none  [local(): lax.all_to_all(pooled.reshape(owners, samples, pooled.shape[-1]), 'table'...]
    all_gather x2 -> x0, blocking collectives: 3.96 us -> none  [dispatch(): columns = lax.all_gather(arrived[None], 'expert', axis=0, tiled=True)]
  transfers between devices with their start and end apart: 4 -> 3, of which waited for: 3 -> 2; matrix products, arithmetic and copies ran while one was open for 4% -> 3% of each run, Pallas kernels for 0% -> 0%
where the time goes in v1:
time: 233 us
  waiting for transfers between devices  130 us (56%)
  Pallas kernels  51.4 us (22%)
  matrix products  26.8 us (12%)
  between operations  14.3 us (6%)
  other arithmetic  7.56 us (3%)
  local copies, waits for them, and re-layouts  2.37 us (1%)
    reduce_scatter x1, waiting for transfers between devices, local(): lax.psum_scatter(weighted, 'table', scatter_dimension=0, tiled=True)  80.3 us
    pallas_call x4, Pallas kernels, exchange(): pl.pallas_call(functools.partial(exchange_kernel, owners, columns, shared...  51.4 us
    all_gather x1, waiting for transfers between devices, local(): lax.all_gather(summed_grad.astype(jnp.bfloat16), 'table', axis=0, tiled=T...  49.9 us
  transfers between devices with their start and end apart: 3, of which 2 were waited for; matrix products, arithmetic and copies ran while one was open for 3% of the time, Pallas kernels for 0%

profile of v1, /device:TPU:0, one launch (start us, length us, event | category | flops | bytes accessed | tf_op | source)
XLA Modules:
  0.0 232.8 jit_solution(10309041532751012190)
XLA Ops:
  7.2 0.0 copy-start
  7.2 0.0 copy-start.11
  7.2 0.0 copy-start.5
  7.2 0.0 reduce-scatter.2.cloned.1.call-start
  7.3 0.9 bitcast_select_fusion
  8.2 2.1 convert_reduce_fusion
  10.3 0.8 constant_dynamic-slice_fusion.1
  11.1 2.8 %fusion.2 = bf16[2048,256]{1,0:T(8,128)(2,1)} fusion(f32[256]{0:T(256)S(1)} %bitcast.96, bf16[256,2048]{1,0:T(8,128)(2,1)S(1)} %convert_reduce_fusion, bf16[1,512,256]{2,1,0:T(8,128)(2,1)} %param.13, f32[512]{0:T(512)} %bitcast.98, s32[256]{0:T(256)} %bitcast.99), kind=kOutput, calls=%fused_computation.10 | convolution fusion | flops 338362368 | bytes 2363392 | tf_op jit(solution)/shard_map/dot_general | solution.py:157
  13.9 0.0 reduce-scatter.2.cloned.1.call-update
  13.9 0.0 all-gather.2.cloned.1.call-start
  13.9 0.2 fusion.8
  14.1 80.3 %reduce-scatter.2.cloned.1.call-done = bf16[128,256]{1,0:T(8,128)(2,1)} async-done(((bf16[2048,256]{1,0:T(8,128)(2,1)}), bf16[128,256]{1,0:T(8,128)(2,1)}) %reduce-scatter.2.cloned.1.call-update) | async-done | bytes 65552 | tf_op jit(solution)/shard_map/reduce_scatter | solution.py:160
  94.5 0.9 fusion.42
  95.4 1.7 convolution_convert_fusion.6
  97.2 12.7 %shard_map.156 = bf16[32,16,256]{2,1,0:T(8,128)(2,1)} custom-call(bf16[16,16,256]{2,1,0:T(8,128)(2,1)} %bitcast.88), custom_call_target="tpu_custom_call" | custom-call | tf_op jit(solution)/shard_map/pallas_call | solution.py:75
  109.9 0.0 copy-start.7
  109.9 4.2 %multiply_convert_fusion.1 = (bf16[512,2048]{1,0:T(8,128)(2,1)S(1)}, f32[512,2048]{1,0:T(8,128)}) fusion(bf16[512,256]{1,0:T(8,128)(2,1)} %bitcast.85, bf16[1,256,2048]{2,1,0:T(8,128)(2,1)S(1)} %copy-done), kind=kOutput, calls=%fused_computation.3 | convolution fusion | flops 542113792 | bytes 7602176 | tf_op jit(solution)/shard_map/dot_general | solution.py:179
  114.2 0.0 copy-done.2
  114.2 0.0 copy-start.6
  114.2 0.0 copy-start.8
  114.2 1.4 convolution_convert_fusion.3
  115.6 12.8 %shard_map.157 = bf16[32,16,256]{2,1,0:T(8,128)(2,1)} custom-call(bf16[32,16,256]{2,1,0:T(8,128)(2,1)} %bitcast.92), custom_call_target="tpu_custom_call" | custom-call | tf_op jit(solution)/shard_map/pallas_call | solution.py:75
  128.4 1.0 convert_element_type.137
  129.5 0.0 copy-done.3
  129.5 0.0 copy-done.9
  129.5 0.0 copy-done.8
  129.5 0.5 multiply_reduce_fusion
  130.1 0.3 fusion.5
  130.4 0.8 convolution_convert_fusion.5
  131.2 12.7 %shard_map.158 = bf16[32,16,256]{2,1,0:T(8,128)(2,1)} custom-call(bf16[16,16,256]{2,1,0:T(8,128)(2,1)} %bitcast.89), custom_call_target="tpu_custom_call" | custom-call | tf_op jit(solution)/shard_map/pallas_call | solution.py:75
  144.0 4.3 %multiply_convert_fusion = bf16[512,2048]{1,0:T(8,128)(2,1)S(1)} fusion(f32[512,2048]{1,0:T(8,128)} %get-tuple-element.18, bf16[512,256]{1,0:T(8,128)(2,1)} %bitcast.90, bf16[1,2048,256]{2,1,0:T(8,128)(2,1)} %param.22), kind=kOutput, calls=%fused_computation.2 | convolution fusion | flops 546308096 | bytes 7602176 | tf_op jit(solution)/shard_map/dot_general | solution.py:204
  148.3 1.4 convolution_convert_fusion.2
  149.7 13.1 %shard_map.159 = bf16[32,16,256]{2,1,0:T(8,128)(2,1)} custom-call(bf16[32,16,256]{2,1,0:T(8,128)(2,1)} %bitcast.93), custom_call_target="tpu_custom_call" | custom-call | tf_op jit(solution)/shard_map/pallas_call | solution.py:75
  162.8 1.0 convert_element_type.147
  163.8 0.0 copy-start.10
  163.9 0.3 fusion.43
  164.2 0.7 fusion.41
  164.9 0.0 all-gather.2.cloned.1.call-update
  165.0 0.6 copy.18
  165.5 3.7 %convolution_bitcast_fusion = f32[1,2048,256]{2,1,0:T(8,128)} fusion(bf16[512,2048]{1,0:T(8,128)(2,1)} %copy-done.12, bf16[512,256]{1,0:T(8,128)(2,1)} %bitcast.91), kind=kOutput, calls=%fused_computation.5 | convolution fusion | flops 536870912 | bytes 4456448 | tf_op jit(solution)/shard_map/dot_general | solution.py:208
  169.2 49.9 %all-gather.2.cloned.1.call-done = bf16[2048,256]{1,0:T(8,128)(2,1)} async-done(((bf16[128,256]{1,0:T(8,128)(2,1)}), bf16[2048,256]{1,0:T(8,128)(2,1)}) %all-gather.2.cloned.1.call-update) | async-done | bytes 1048592 | tf_op jit(solution)/shard_map/all_gather | solution.py:226
  219.1 0.0 copy-done.10
  219.1 3.0 %convolution_convert_fusion.1 = bf16[512,256]{1,0:T(8,128)(2,1)} fusion(bf16[2048,256]{1,0:T(8,128)(2,1)} %all-gather.2.cloned.1.call-done, bf16[256,2048]{1,0:T(8,128)(2,1)} %copy-done.2, s32[256]{0:T(256)S(1)} %bitcast.100, f32[256]{0:T(256)S(1)} %bitcast.97), kind=kOutput, calls=%fused_computation.11 | convolution fusion | flops 335937536 | bytes 2361344 | tf_op jit(solution)/shard_map/dot_general | solution.py:228
  222.1 1.0 constant_dynamic-slice_fusion
  223.1 0.1 collective-permute-start
  223.2 2.0 convolution_bitcast_fusion.1
  225.3 0.0 collective-permute-done
  225.3 0.7 add_bitcast_fusion
  (21 shorter events, 0.1 us)
Async XLA Ops:
  7.2 102.8 %copy-start = (bf16[1,256,2048]{2,1,0:T(8,128)(2,1)S(1)}, bf16[1,256,2048]{2,1,0:T(8,128)(2,1)}, u32[]{:S(2)}) copy-start(bf16[1,256,2048]{2,1,0:T(8,128)(2,1)} %param.21) | copy-start | bytes 3145732
  7.2 6.8 %copy-start.11 = (s32[1,128,1]{1,2,0:T(1,128)S(1)}, s32[1,128,1]{1,2,0:T(1,128)}, u32[]{:S(2)}) copy-start(s32[1,128,1]{1,2,0:T(1,128)} %param.20) | copy-start | bytes 1540
  7.2 88.2 %copy-start.5 = (f32[256]{0:T(256)S(1)}, f32[256]{0:T(256)}, u32[]{:S(2)}) copy-start(f32[256]{0:T(256)} %param.19) | copy-start | bytes 3076
  7.2 87.3 %reduce-scatter.2.cloned.1.call-start = ((), (), s32[]{:S(2)}) async-start(), calls=%async_computation.1 | async-start | bytes 1114112 | tf_op jit(solution)/shard_map/reduce_scatter | solution.py:160
  10.3 103.9 %copy-start.2 = (bf16[256,2048]{1,0:T(8,128)(2,1)}, bf16[256,2048]{1,0:T(8,128)(2,1)S(1)}, u32[]{:S(2)}) copy-start(bf16[256,2048]{1,0:T(8,128)(2,1)S(1)} %convert_reduce_fusion) | copy-start | bytes 3145732
  13.9 205.2 %all-gather.2.cloned.1.call-start = ((), (), s32[]{:S(2)}) async-start(), calls=%async_computation.2 | async-start | bytes 1114112 | tf_op jit(solution)/shard_map/all_gather | solution.py:226
  109.9 4.2 %copy-start.7 = (bf16[1,2048,256]{2,1,0:T(8,128)(2,1)S(1)}, bf16[1,2048,256]{2,1,0:T(8,128)(2,1)}, u32[]{:S(2)}) copy-start(bf16[1,2048,256]{2,1,0:T(8,128)(2,1)} %param.22) | copy-start | bytes 3145732
  114.2 1.5 copy-start.12
  114.2 15.3 %copy-start.3 = (bf16[128,256]{1,0:T(8,128)(2,1)S(1)}, bf16[128,256]{1,0:T(8,128)(2,1)}, u32[]{:S(2)}) copy-start(bf16[128,256]{1,0:T(8,128)(2,1)} %reduce-scatter.2.cloned.1.call-done) | copy-start | bytes 196612
  114.2 15.3 %copy-start.9 = (f32[3,256]{1,0:T(4,128)S(1)}, f32[3,256]{1,0:T(4,128)}, u32[]{:S(2)}) copy-start(f32[3,256]{1,0:T(4,128)} %param.24) | copy-start | bytes 9220
  114.2 15.9 %copy-start.6 = (f32[1,128,3]{1,0,2:T(1,128)S(1)}, f32[1,128,3]{1,0,2:T(1,128)}, u32[]{:S(2)}) copy-start(f32[1,128,3]{1,0,2:T(1,128)} %param.25) | copy-start | bytes 4612
  114.2 15.3 %copy-start.8 = (bf16[3,256,256]{2,1,0:T(8,128)(2,1)S(1)}, bf16[3,256,256]{2,1,0:T(8,128)(2,1)}, u32[]{:S(2)}) copy-start(bf16[3,256,256]{2,1,0:T(8,128)(2,1)} %param.23) | copy-start | bytes 1179652
  163.8 55.3 %copy-start.10 = (s32[1,1,256]{2,1,0:T(1,128)S(1)}, s32[1,1,256]{2,1,0:T(1,128)}, u32[]{:S(2)}) copy-start(s32[1,1,256]{2,1,0:T(1,128)} %param.15) | copy-start | bytes 3076
  165.5 57.7 %copy-start.1 = (bf16[32,16,256]{2,1,0:T(8,128)(2,1)S(1)}, bf16[32,16,256]{2,1,0:T(8,128)(2,1)}, u32[]{:S(2)}) copy-start(bf16[32,16,256]{2,1,0:T(8,128)(2,1)} %shard_map.156) | copy-start | bytes 786436
  222.1 3.1 %copy-start.4 = (bf16[512,256]{1,0:T(8,128)(2,1)S(1)}, bf16[512,256]{1,0:T(8,128)(2,1)}, u32[]{:S(2)}) copy-start(bf16[512,256]{1,0:T(8,128)(2,1)} %convolution_convert_fusion.1) | copy-start | bytes 786436
  223.1 2.1 collective-permute-start
Sparse Core Ops, SparseCore 0:
  14.0 80.4 reduce-scatter.1
  165.1 54.0 all-gather.1

commit v2 on v1

--- a/solution.py
+++ b/solution.py
@@ -23,76 +23,226 @@
     return jnp.sum(hits, axis=0).astype(jnp.bfloat16)
 
 
-def exchange_kernel(owners, columns, shared, x_ref, o_ref, send_sem, recv_sem, own_sem):
-    devices = owners * columns
-    mine = lax.axis_index("expert") * owners + lax.axis_index("table")
+def here():
+    return lax.axis_index("table"), lax.axis_index("expert")
+
+
+def remote(src, dst, send_sem, recv_sem, slot, device):
+    return pltpu.make_async_remote_copy(
+        src_ref=src,
+        dst_ref=dst,
+        send_sem=send_sem.at[slot],
+        recv_sem=recv_sem.at[slot],
+        device_id=device,
+        device_id_type=pl.DeviceIdType.MESH,
+    )
+
+
+def meet(peers):
     barrier = pltpu.get_barrier_semaphore()
-
-    def place(step):
-        other = lax.rem(mine + step, devices)
-        return other, lax.rem(other, owners), lax.div(other, owners)
-
-    def greet(step, carry):
-        _, row, column = place(step)
-        pl.semaphore_signal(
-            barrier, inc=1, device_id=(row, column), device_id_type=pl.DeviceIdType.MESH
-        )
-        return carry
-
-    def copy(step):
-        other, row, column = place(step)
-        return pltpu.make_async_remote_copy(
-            src_ref=x_ref.at[row if shared else other],
-            dst_ref=o_ref.at[mine],
-            send_sem=send_sem.at[step],
-            recv_sem=recv_sem.at[step],
-            device_id=(row, column),
-            device_id_type=pl.DeviceIdType.MESH,
-        )
-
-    def send(step, carry):
-        copy(step).start()
-        return carry
-
-    def settle(step, carry):
-        copy(step).wait()
-        return carry
-
-    lax.fori_loop(1, devices, greet, 0)
-    own = pltpu.make_async_copy(
-        x_ref.at[lax.axis_index("table") if shared else mine], o_ref.at[mine], own_sem
-    )
+    for peer in peers:
+        pl.semaphore_signal(barrier, inc=1, device_id=peer, device_id_type=pl.DeviceIdType.MESH)
+    pl.semaphore_wait(barrier, len(peers))
+
+
+def dispatch_kernel(owners, x_ref, o_ref, send_sem, recv_sem, own_sem):
+    row, column = here()
+    sibling = (row, 1 - column)
+    peers = [(lax.rem(row + step, owners), column) for step in range(1, owners)]
+    own = pltpu.make_async_copy(x_ref.at[row], o_ref.at[column, row], own_sem)
     own.start()
-    pl.semaphore_wait(barrier, devices - 1)
-    lax.fori_loop(1, devices, send, 0)
+    meet(peers + [sibling])
+    copies = [
+        remote(x_ref.at[peer[0]], o_ref.at[column, row], send_sem, recv_sem, i, peer)
+        for i, peer in enumerate(peers)
+    ]
+    for copy in copies:
+        copy.start()
     own.wait()
-    lax.fori_loop(1, devices, settle, 0)
-
-
-def exchange(blocks, shared, collective_id):
-    owners, columns = lax.axis_size("table"), lax.axis_size("expert")
-    devices = owners * columns
+    for copy in copies:
+        copy.wait_recv()
+    across = remote(
+        o_ref.at[column], o_ref.at[column], send_sem, recv_sem, owners - 1, sibling
+    )
+    across.start()
+    for copy in copies:
+        copy.wait_send()
+    across.wait()
+
+
+def return_kernel(owners, x_ref, o_ref, theirs, total, send_sem, recv_sem, own_sem):
+    row, column = here()
+    sibling = (row, 1 - column)
+    peers = [(lax.rem(row + step, owners), column) for step in range(1, owners)]
+    meet(peers + [sibling])
+    across = remote(x_ref.at[1 - column], theirs, send_sem, recv_sem, owners - 1, sibling)
+    across.start()
+    across.wait_recv()
+    total[...] = (
+        x_ref[column].astype(jnp.float32) + theirs[...].astype(jnp.float32)
+    ).astype(total.dtype)
+    copies = [
+        remote(total.at[peer[0]], o_ref.at[row], send_sem, recv_sem, i, peer)
+        for i, peer in enumerate(peers)
+    ]
+    for copy in copies:
+        copy.start()
+    own = pltpu.make_async_copy(total.at[row], o_ref.at[row], own_sem)
+    own.start()
+    across.wait_send()
+    own.wait()
+    for copy in copies:
+        copy.wait()
+
+
+def plane_of(row):
+    layer, y, x = lax.div(row, 4), lax.rem(lax.div(row, 2), 2), lax.rem(row, 2)
+    return layer, y, x
+
+
+def place(layer, y, x):
+    return layer * 4 + y * 2 + x
+
+
+def scatter_kernel(x_ref, o_ref, diagonal, staged, arrived, up, down, send_sem, recv_sem):
+    row, column = here()
+    z, y, x = plane_of(row)
+    beside, above = (place(z, y, 1 - x), column), (place(z, 1 - y, x), column)
+    layers = [lax.rem(z + s, 4) for s in range(4)]
+    meet([beside, above] + [(place(layers[s], y, x), column) for s in (1, 2, 3)])
+    half = x_ref.shape[1] // 2
+    first, last = pl.ds(0, half), pl.ds(half, half)
+    turns = (2, 1, 3, 0)
+    sent = []
+    corner = {}
+    for s in turns:
+        target = x_ref.at[place(layers[s], 1 - y, 1 - x)]
+        corner[s] = (
+            remote(target.at[first], diagonal.at[s, 0], send_sem, recv_sem, s * 5, beside),
+            remote(target.at[last], diagonal.at[s, 1], send_sem, recv_sem, s * 5 + 1, above),
+        )
+        for copy in corner[s]:
+            copy.start()
+            sent.append(copy)
+    side = {}
+    for s in turns:
+        to_beside, to_above = place(layers[s], y, 1 - x), place(layers[s], 1 - y, x)
+        corner[s][0].wait_recv()
+        staged[s, 1, first] = (
+            x_ref[to_above, first].astype(jnp.float32) + diagonal[s, 0].astype(jnp.float32)
+        ).astype(staged.dtype)
+        staged[s, 1, last] = x_ref[to_above, last]
+        corner[s][1].wait_recv()
+        staged[s, 0, first] = x_ref[to_beside, first]
+        staged[s, 0, last] = (
+            x_ref[to_beside, last].astype(jnp.float32) + diagonal[s, 1].astype(jnp.float32)
+        ).astype(staged.dtype)
+        side[s] = (
+            remote(staged.at[s, 0], arrived.at[s, 0], send_sem, recv_sem, s * 5 + 2, beside),
+            remote(staged.at[s, 1], arrived.at[s, 1], send_sem, recv_sem, s * 5 + 3, above),
+        )
+        for copy in side[s]:
+            copy.start()
+            sent.append(copy)
+    vertical = {}
+    for s in turns:
+        for copy in side[s]:
+            copy.wait_recv()
+        partial = (
+            x_ref[place(layers[s], y, x)].astype(jnp.float32)
+            + arrived[s, 0].astype(jnp.float32)
+            + arrived[s, 1].astype(jnp.float32)
+        )
+        if s == 0:
+            o_ref[...] = partial
+        else:
+            up[s] = partial.astype(up.dtype)
+            vertical[s] = remote(
+                up.at[s], down.at[s], send_sem, recv_sem, s * 5 + 4, (place(layers[s], y, x), column)
+            )
+            vertical[s].start()
+            sent.append(vertical[s])
+    for s in turns[:3]:
+        vertical[s].wait_recv()
+        o_ref[...] += down[s].astype(jnp.float32)
+    for copy in sent:
+        copy.wait_send()
+
+
+def gather_kernel(x_ref, o_ref, send_sem, recv_sem, own_sem):
+    row, column = here()
+    z, y, x = plane_of(row)
+    beside, above = (place(z, y, 1 - x), column), (place(z, 1 - y, x), column)
+    own = pltpu.make_async_copy(x_ref, o_ref.at[row], own_sem)
+    own.start()
+    meet([beside, above] + [(place(lax.rem(z + s, 4), y, x), column) for s in (1, 2, 3)])
+    half = x_ref.shape[0] // 2
+    first, last = pl.ds(0, half), pl.ds(half, half)
+    sent = []
+
+    def send(src, dst, slot, device):
+        copy = remote(src, dst, send_sem, recv_sem, slot, device)
+        copy.start()
+        sent.append(copy)
+        return copy
+
+    vertical = {
+        s: send(x_ref, o_ref.at[row], s * 5, (place(lax.rem(z + s, 4), y, x), column))
+        for s in (1, 3, 2)
+    }
+    turns = (0, 1, 3, 2)
+    side = {}
+    for s in turns:
+        mine = place(lax.rem(z + 4 - s, 4), y, x)
+        source = x_ref
+        if s > 0:
+            vertical[s].wait_recv()
+            source = o_ref.at[mine]
+        side[s] = (
+            send(source, o_ref.at[mine], s * 5 + 1, beside),
+            send(source, o_ref.at[mine], s * 5 + 2, above),
+        )
+    corner = []
+    for s in turns:
+        layer = lax.rem(z + 4 - s, 4)
+        side[s][0].wait_recv()
+        block = o_ref.at[place(layer, y, 1 - x), first]
+        corner.append(send(block, block, s * 5 + 3, above))
+        side[s][1].wait_recv()
+        block = o_ref.at[place(layer, 1 - y, x), last]
+        corner.append(send(block, block, s * 5 + 4, beside))
+    for copy in corner:
+        copy.wait_recv()
+    own.wait()
+    for copy in sent:
+        copy.wait_send()
+
+
+def call(kernel, operand, shape, dtype, scratch, copies, collective_id):
+    semaphores = [pltpu.SemaphoreType.DMA((copies,)), pltpu.SemaphoreType.DMA((copies,))]
     return pl.pallas_call(
-        functools.partial(exchange_kernel, owners, columns, shared),
-        out_shape=jax.ShapeDtypeStruct((devices,) + blocks.shape[1:], blocks.dtype),
+        kernel,
+        out_shape=jax.ShapeDtypeStruct(shape, dtype),
         in_specs=[pl.BlockSpec(memory_space=pltpu.VMEM)],
         out_specs=pl.BlockSpec(memory_space=pltpu.VMEM),
-        scratch_shapes=[
-            pltpu.SemaphoreType.DMA((devices,)),
-            pltpu.SemaphoreType.DMA((devices,)),
-            pltpu.SemaphoreType.DMA,
-        ],
-        compiler_params=pltpu.CompilerParams(collective_id=collective_id, has_side_effects=True),
-    )(blocks)
+        scratch_shapes=[pltpu.VMEM(s, jnp.bfloat16) for s in scratch] + semaphores
+        + ([] if kernel is scatter_kernel else [pltpu.SemaphoreType.DMA]),
+        compiler_params=pltpu.CompilerParams(
+            collective_id=collective_id, has_side_effects=True, vmem_limit_bytes=32 << 20
+        ),
+    )(operand)
 
 
 def direct():
-    return lax.axis_size("expert") == 2
+    return lax.axis_size("expert") == 2 and lax.axis_size("table") == 16
 
 
 def dispatch(buffer, collective_id):
     if direct():
-        return exchange(buffer, True, collective_id).reshape(-1, buffer.shape[-1])
+        owners = buffer.shape[0]
+        kernel = functools.partial(dispatch_kernel, owners)
+        arrived = call(kernel, buffer, (2,) + buffer.shape, buffer.dtype, (), owners, collective_id)
+        return arrived.reshape(-1, buffer.shape[-1])
     arrived = lax.all_to_all(buffer, "table", split_axis=0, concat_axis=0, tiled=True)
     columns = lax.all_gather(arrived[None], "expert", axis=0, tiled=True)
     return columns.reshape(-1, buffer.shape[-1])
@@ -102,14 +252,47 @@
     width = partial.shape[-1]
     partial = partial.astype(jnp.bfloat16)
     if direct():
-        arrived = exchange(partial.reshape(-1, capacity, width), False, collective_id)
-        arrived = arrived.reshape(2, experts * capacity, width).astype(jnp.float32)
-        return (arrived[0] + arrived[1]).astype(jnp.bfloat16)
+        block = (experts, capacity, width)
+        kernel = functools.partial(return_kernel, experts)
+        arrived = call(
+            kernel,
+            partial.reshape((2,) + block),
+            block,
+            partial.dtype,
+            (block, block),
+            experts,
+            collective_id,
+        )
+        return arrived.reshape(experts * capacity, width)
     summed = lax.psum_scatter(partial, "expert", scatter_dimension=0, tiled=True)
     arrived = lax.all_to_all(
         summed.reshape(experts, capacity, width), "table", split_axis=0, concat_axis=0, tiled=True
     )
     return arrived.reshape(experts * capacity, width)
+
+
+def sum_features(weighted, samples):
+    width = weighted.shape[-1]
+    if direct():
+        block = (samples, width)
+        return call(
+            scatter_kernel,
+            weighted.reshape(-1, samples, width),
+            block,
+            jnp.float32,
+            ((4, 2, samples // 2, width), (4, 2) + block, (4, 2) + block, (4,) + block, (4,) + block),
+            20,
+            5,
+        )
+    return lax.psum_scatter(weighted, "table", scatter_dimension=0, tiled=True).astype(jnp.float32)
+
+
+def gather_rows(rows):
+    if direct():
+        owners = lax.axis_size("table")
+        gathered = call(gather_kernel, rows, (owners,) + rows.shape, rows.dtype, (), 20, 6)
+        return gathered.reshape(-1, rows.shape[-1])
+    return lax.all_gather(rows, "table", axis=0, tiled=True)
 
 
 def sum_rows(row_grad):
@@ -157,9 +340,7 @@
     pooled = lax.dot_general(counts, dequant, contract_rows, preferred_element_type=jnp.float32)
     own_gain = lax.dynamic_slice_in_dim(feat_gain, lax.axis_index("table"), 1, 0)
     weighted = (pooled.astype(jnp.bfloat16).astype(jnp.float32) * own_gain).astype(jnp.bfloat16)
-    summed = lax.psum_scatter(weighted, "table", scatter_dimension=0, tiled=True).astype(
-        jnp.float32
-    )
+    summed = sum_features(weighted, samples)
     inverse = lax.rsqrt(jnp.mean(summed * summed, axis=-1, keepdims=True) + 1e-05)
     normed = (summed * inverse * norm_gain).astype(jnp.bfloat16)
     chosen = expert_ids[0, :, 0]
@@ -223,7 +404,7 @@
         scaled_grad
         - summed * inverse * inverse * jnp.mean(scaled_grad * summed, axis=-1, keepdims=True)
     )
-    returned = lax.all_gather(summed_grad.astype(jnp.bfloat16), "table", axis=0, tiled=True)
+    returned = gather_rows(summed_grad.astype(jnp.bfloat16))
     window_grad = jnp.dot(counts, returned, preferred_element_type=jnp.float32) * own_gain
     row_grad = jnp.dot(
         row_select, window_grad.astype(jnp.bfloat16), preferred_element_type=jnp.float32

time: 233 us -> 107 us (0.46)
  waiting for transfers between devices: 130 us -> 0.01 us
  Pallas kernels: 51.4 us -> 75.1 us
  between operations: 14.3 us -> 0.93 us
  matrix products: 26.8 us -> 23.8 us
  other arithmetic: 7.56 us -> 4.62 us
    reduce_scatter x1 -> x0, waiting for transfers between devices: 80.3 us -> none  [local(): lax.psum_scatter(weighted, 'table', scatter_dimension=0, tiled=True)]
    all_gather x1 -> x0, waiting for transfers between devices: 49.9 us -> none  [local(): lax.all_gather(summed_grad.astype(jnp.bfloat16), 'table', axis=0, tiled=T...]
    pallas_call x4 -> x6, Pallas kernels: 51.4 us -> 75.1 us  [call(): pl.pallas_call(kernel, out_shape=jax.ShapeDtypeStruct(shape, dtype), in_s...]
    convert_element_type x5 -> x1, other arithmetic: 2.81 us -> 0.11 us  [local(): returned = gather_rows(summed_grad.astype(jnp.bfloat16))]
  transfers between devices with their start and end apart: 3 -> 1, of which waited for: 2 -> 0; matrix products, arithmetic and copies ran while one was open for 3% -> 7% of each run, Pallas kernels for 0% -> 0%
where the time goes in v2:
time: 107 us
  Pallas kernels  75.1 us (70%)
  matrix products  23.8 us (22%)
  other arithmetic  4.62 us (4%)
  local copies, waits for them, and re-layouts  2.45 us (2%)
    pallas_call x6, Pallas kernels, call(): pl.pallas_call(kernel, out_shape=jax.ShapeDtypeStruct(shape, dtype), in_s...  75.1 us
    dot_general x1, matrix products, local(): lax.dot_general(gathered_grad, weight_out, contract_cols, preferred_eleme...  3.91 us
    dot_general x1, matrix products, local(): lax.dot_general(hidden, gathered_grad, contract_rows, preferred_element_t...  3.65 us
    dot_general x1, matrix products, local(): lax.dot_general(gathered, grad_pre, contract_rows, preferred_element_type...  3.64 us
    dot_general x1, matrix products, local(): pre_act = jnp.dot(gathered, weight_in, preferred_element_type=jnp.float32)  3.18 us
  transfers between devices with their start and end apart: 1, of which 0 were waited for; matrix products, arithmetic and copies ran while one was open for 7% of the time, Pallas kernels for 0%

profile of v2, /device:TPU:0, one launch (start us, length us, event | category | flops | bytes accessed | tf_op | source)
XLA Modules:
  0.0 107.0 jit_solution(2017367687414456844)
XLA Ops:
  0.6 0.0 copy-start
  0.6 0.0 copy-start.3
  0.7 0.9 fusion.8
  1.6 0.7 convert_add_fusion
  2.2 0.9 bitcast_select_fusion
  3.1 2.1 %convert_reduce_fusion = bf16[256,2048]{1,0:T(8,128)(2,1)S(1)} fusion(s32[8,2048]{1,0:T(8,128)S(1)} %bitcast_select_fusion), kind=kLoop, calls=%fused_computation | loop fusion | flops 12058624 | bytes 1114112 | tf_op jit(solution)/shard_map/reduce_sum | solution.py:23
  5.2 0.0 copy-start.2
  5.2 0.8 constant_dynamic-slice_fusion.1
  6.0 1.8 %fusion.2 = bf16[2048,256]{1,0:T(8,128)(2,1)S(1)} fusion(f32[256]{0:T(256)S(1)} %bitcast.100, bf16[256,2048]{1,0:T(8,128)(2,1)S(1)} %convert_reduce_fusion, bf16[1,512,256]{2,1,0:T(8,128)(2,1)} %param.13, f32[512]{0:T(512)} %bitcast.102, s32[256]{0:T(256)} %bitcast.103), kind=kOutput, calls=%fused_computation.10 | convolution fusion | flops 338362368 | bytes 2363392 | tf_op jit(solution)/shard_map/dot_general | solution.py:340
  7.8 18.7 %shard_map.156 = f32[128,256]{1,0:T(8,128)S(1)} custom-call(bf16[16,128,256]{2,1,0:T(8,128)(2,1)S(1)} %bitcast.89), custom_call_target="tpu_custom_call" | custom-call | tf_op jit(solution)/shard_map/pallas_call | solution.py:223
  26.5 0.1 multiply_reduce_fusion.2
  26.6 0.0 copy-done.3
  26.6 0.2 convolution_convert_fusion.6
  26.9 8.9 %shard_map.157 = bf16[2,16,16,256]{3,2,1,0:T(8,128)(2,1)S(1)} custom-call(bf16[16,16,256]{2,1,0:T(8,128)(2,1)S(1)} %bitcast.92), custom_call_target="tpu_custom_call" | custom-call | tf_op jit(solution)/shard_map/pallas_call | solution.py:223
  35.8 0.0 copy-done
  35.8 0.0 copy-start.5
  35.8 3.2 %multiply_convert_fusion.1 = (bf16[512,2048]{1,0:T(8,128)(2,1)S(1)}, f32[512,2048]{1,0:T(8,128)}) fusion(bf16[512,256]{1,0:T(8,128)(2,1)S(1)} %bitcast.87, bf16[1,256,2048]{2,1,0:T(8,128)(2,1)S(1)} %copy-done), kind=kOutput, calls=%fused_computation.3 | convolution fusion | flops 542113792 | bytes 7602176 | tf_op jit(solution)/shard_map/dot_general | solution.py:360
  39.0 0.0 copy-done.2
  39.0 0.0 copy-done.5
  39.0 0.0 copy-start.7
  39.0 0.0 copy-start.6
  39.0 0.7 convolution_convert_fusion.3
  39.7 0.6 copy-done.10
  40.3 10.0 %shard_map.158 = bf16[16,16,256]{2,1,0:T(8,128)(2,1)S(1)} custom-call(bf16[2,16,16,256]{3,2,1,0:T(8,128)(2,1)S(1)} %bitcast.96), custom_call_target="tpu_custom_call" | custom-call | tf_op jit(solution)/shard_map/pallas_call | solution.py:223
  50.3 0.0 copy-done.8
  50.3 0.0 copy-done.7
  50.3 1.1 %multiply_reduce_fusion = (f32[3,128]{1,0:T(4,128)S(1)}, f32[3,128,256]{2,1,0:T(8,128)}) fusion(f32[3,256]{1,0:T(4,128)S(1)} %copy-done.8, bf16[3,256,256]{2,1,0:T(8,128)(2,1)S(1)} %copy-done.7, bf16[256,256]{1,0:T(8,128)(2,1)S(1)} %bitcast.98, s32[128]{0:T(128)S(1)} %convert_add_fusion, f32[256]{0:T(256)S(1)} %copy-done.3, f32[128,256]{1,0:T(8,128)S(1)} %shard_map.156, ...), kind=kOutput, calls=%fused_computation.41 | convolution fusion | flops 67927680 | bytes 1055232 | tf_op jit(solution)/shard_map/be,kem->kbm/dot_general | solution.py:369
  51.4 0.0 copy-done.4
  51.5 1.3 %fusion.5 = bf16[128,256]{1,0:T(8,128)(2,1)S(1)} fusion(bf16[3,256,256]{2,1,0:T(8,128)(2,1)S(1)} %copy-done.7, f32[3,128,256]{2,1,0:T(8,128)} %get-tuple-element.20, f32[3,128]{1,0:T(4,128)S(1)} %get-tuple-element.15, f32[3,256]{1,0:T(4,128)S(1)} %copy-done.8), kind=kOutput, calls=%fused_computation.24 | convolution fusion | flops 51347456 | bytes 856576 | tf_op jit(solution)/shard_map/kbm,kem->be/dot_general | solution.py:378
  52.8 0.2 convolution_convert_fusion.5
  53.0 9.5 %shard_map.159 = bf16[2,16,16,256]{3,2,1,0:T(8,128)(2,1)S(1)} custom-call(bf16[16,16,256]{2,1,0:T(8,128)(2,1)S(1)} %bitcast.93), custom_call_target="tpu_custom_call" | custom-call | tf_op jit(solution)/shard_map/pallas_call | solution.py:223
  62.5 0.0 copy-done.6
  62.5 3.9 %multiply_convert_fusion = bf16[512,2048]{1,0:T(8,128)(2,1)S(1)} fusion(f32[512,2048]{1,0:T(8,128)} %get-tuple-element.18, bf16[512,256]{1,0:T(8,128)(2,1)S(1)} %bitcast.94, bf16[1,2048,256]{2,1,0:T(8,128)(2,1)S(1)} %copy-done.6), kind=kOutput, calls=%fused_computation.2 | convolution fusion | flops 546308096 | bytes 7602176 | tf_op jit(solution)/shard_map/dot_general | solution.py:385
  66.4 0.0 copy-start.1
  66.4 0.0 copy-start.9
  66.4 0.8 convolution_convert_fusion.2
  67.2 0.5 copy-done.1
  67.7 10.2 %shard_map.160 = bf16[16,16,256]{2,1,0:T(8,128)(2,1)S(1)} custom-call(bf16[2,16,16,256]{3,2,1,0:T(8,128)(2,1)S(1)} %bitcast.97), custom_call_target="tpu_custom_call" | custom-call | tf_op jit(solution)/shard_map/pallas_call | solution.py:223
  78.0 0.3 multiply_reduce_fusion.1
  78.3 0.1 multiply_convert_fusion.4.x_ref
  78.4 17.9 %shard_map.161 = bf16[16,128,256]{2,1,0:T(8,128)(2,1)S(1)} custom-call(bf16[128,256]{1,0:T(8,128)(2,1)S(1)} %multiply_convert_fusion.4.x_ref), custom_call_target="tpu_custom_call" | custom-call | tf_op jit(solution)/shard_map/pallas_call | solution.py:223
  96.3 2.0 %convolution_convert_fusion.1 = bf16[512,256]{1,0:T(8,128)(2,1)S(1)} fusion(bf16[2048,256]{1,0:T(8,128)(2,1)S(1)} %bitcast.90, bf16[256,2048]{1,0:T(8,128)(2,1)} %copy-done.2, s32[256]{0:T(256)S(1)} %bitcast.104, f32[256]{0:T(256)S(1)} %bitcast.101), kind=kOutput, calls=%fused_computation.11 | convolution fusion | flops 335937536 | bytes 2361344 | tf_op jit(solution)/shard_map/dot_general | solution.py:409
  98.3 0.1 collective-permute-start
  98.4 3.7 %convolution_bitcast_fusion = f32[1,2048,256]{2,1,0:T(8,128)} fusion(bf16[512,2048]{1,0:T(8,128)(2,1)} %copy-done.10, bf16[512,256]{1,0:T(8,128)(2,1)S(1)} %bitcast.95), kind=kOutput, calls=%fused_computation.5 | convolution fusion | flops 536870912 | bytes 4456448 | tf_op jit(solution)/shard_map/dot_general | solution.py:389
  102.0 0.6 copy.18
  102.6 3.6 %convolution_bitcast_fusion.1 = f32[1,256,2048]{2,1,0:T(8,128)} fusion(bf16[512,256]{1,0:T(8,128)(2,1)S(1)} %bitcast.88, bf16[512,2048]{1,0:T(8,128)(2,1)} %copy-done.1), kind=kOutput, calls=%fused_computation.6 | convolution fusion | flops 536870912 | bytes 4456448 | tf_op jit(solution)/shard_map/dot_general | solution.py:392
  106.3 0.0 collective-permute-done
  106.3 0.7 add_bitcast_fusion
  (9 shorter events, 0.1 us)
Async XLA Ops:
  0.6 35.1 %copy-start = (bf16[1,256,2048]{2,1,0:T(8,128)(2,1)S(1)}, bf16[1,256,2048]{2,1,0:T(8,128)(2,1)}, u32[]{:S(2)}) copy-start(bf16[1,256,2048]{2,1,0:T(8,128)(2,1)} %param.21) | copy-start | bytes 3145732
  0.6 26.0 %copy-start.3 = (f32[256]{0:T(256)S(1)}, f32[256]{0:T(256)}, u32[]{:S(2)}) copy-start(f32[256]{0:T(256)} %param.19) | copy-start | bytes 3076
  5.2 33.8 %copy-start.2 = (bf16[256,2048]{1,0:T(8,128)(2,1)}, bf16[256,2048]{1,0:T(8,128)(2,1)S(1)}, u32[]{:S(2)}) copy-start(bf16[256,2048]{1,0:T(8,128)(2,1)S(1)} %convert_reduce_fusion) | copy-start | bytes 3145732
  35.8 3.2 %copy-start.5 = (bf16[1,2048,256]{2,1,0:T(8,128)(2,1)S(1)}, bf16[1,2048,256]{2,1,0:T(8,128)(2,1)}, u32[]{:S(2)}) copy-start(bf16[1,2048,256]{2,1,0:T(8,128)(2,1)} %param.22) | copy-start | bytes 3145732
  39.0 1.3 %copy-start.10 = (bf16[512,2048]{1,0:T(8,128)(2,1)}, bf16[512,2048]{1,0:T(8,128)(2,1)S(1)}, u32[]{:S(2)}) copy-start(bf16[512,2048]{1,0:T(8,128)(2,1)S(1)} %get-tuple-element.17) | copy-start | bytes 6291460
  39.0 11.3 %copy-start.8 = (f32[3,256]{1,0:T(4,128)S(1)}, f32[3,256]{1,0:T(4,128)}, u32[]{:S(2)}) copy-start(f32[3,256]{1,0:T(4,128)} %param.24) | copy-start | bytes 9220
  39.0 12.5 %copy-start.4 = (f32[1,128,3]{1,0,2:T(1,128)S(1)}, f32[1,128,3]{1,0,2:T(1,128)}, u32[]{:S(2)}) copy-start(f32[1,128,3]{1,0,2:T(1,128)} %param.25) | copy-start | bytes 4612
  39.0 11.3 %copy-start.7 = (bf16[3,256,256]{2,1,0:T(8,128)(2,1)S(1)}, bf16[3,256,256]{2,1,0:T(8,128)(2,1)}, u32[]{:S(2)}) copy-start(bf16[3,256,256]{2,1,0:T(8,128)(2,1)} %param.23) | copy-start | bytes 1179652
  39.0 23.5 %copy-start.6 = (bf16[1,2048,256]{2,1,0:T(8,128)(2,1)S(1)}, bf16[1,2048,256]{2,1,0:T(8,128)(2,1)}, u32[]{:S(2)}) copy-start(bf16[1,2048,256]{2,1,0:T(8,128)(2,1)} %param.22) | copy-start | bytes 3145732
  66.4 1.3 %copy-start.1 = (bf16[512,2048]{1,0:T(8,128)(2,1)}, bf16[512,2048]{1,0:T(8,128)(2,1)S(1)}, u32[]{:S(2)}) copy-start(bf16[512,2048]{1,0:T(8,128)(2,1)S(1)} %multiply_convert_fusion) | copy-start | bytes 6291460
  66.4 29.9 %copy-start.9 = (s32[1,1,256]{2,1,0:T(1,128)S(1)}, s32[1,1,256]{2,1,0:T(1,128)}, u32[]{:S(2)}) copy-start(s32[1,1,256]{2,1,0:T(1,128)} %param.15) | copy-start | bytes 3076
  98.3 7.9 %collective-permute-start = (bf16[256,256]{1,0:T(8,128)(2,1)S(1)}, bf16[256,256]{1,0:T(8,128)(2,1)S(1)}, u32[]{:S(2)}, u32[]{:S(2)}) collective-permute-start(bf16[256,256]{1,0:T(8,128)(2,1)S(1)} %constant_dynamic-slice_fusion), channel_id=1, source_target_pairs={{0,1},{1,0},{2,3},{3,2},{4,5},{5,4},{6,7},{7,6},{8,9},{9,8},{10,11... | collective-permute-start | bytes 393224 | tf_op jit(solution)/shard_map/ppermute | solution.py:305

commit v3 on v2

--- a/solution.py
+++ b/solution.py
@@ -45,54 +45,204 @@
     pl.semaphore_wait(barrier, len(peers))
 
 
-def dispatch_kernel(owners, x_ref, o_ref, send_sem, recv_sem, own_sem):
+def experts_kernel(
+    normed_ref,
+    placing_ref,
+    placed_ref,
+    w_in_ref,
+    w_out_ref,
+    tow1_ref,
+    tow2_ref,
+    targets_ref,
+    predicted_ref,
+    normed_grad_ref,
+    grad_in_ref,
+    grad_out_ref,
+    outgoing,
+    rows,
+    partial,
+    theirs,
+    total,
+    arrived,
+    hidden,
+    slope,
+    grad_pre,
+    send_sem,
+    recv_sem,
+):
+    owners, capacity, width = outgoing.shape[1:]
+    count = owners * capacity
     row, column = here()
     sibling = (row, 1 - column)
     peers = [(lax.rem(row + step, owners), column) for step in range(1, owners)]
-    own = pltpu.make_async_copy(x_ref.at[row], o_ref.at[column, row], own_sem)
-    own.start()
-    meet(peers + [sibling])
-    copies = [
-        remote(x_ref.at[peer[0]], o_ref.at[column, row], send_sem, recv_sem, i, peer)
-        for i, peer in enumerate(peers)
-    ]
-    for copy in copies:
+    units = w_in_ref.shape[1]
+    tile = 512
+    contract_rows = (((0,), (0,)), ((), ()))
+    contract_cols = (((1,), (1,)), ((), ()))
+    sent = []
+
+    def product(left, right, dims=(((1,), (0,)), ((), ()))):
+        return lax.dot_general(left, right, dims, preferred_element_type=jnp.float32)
+
+    def part(step):
+        return pl.ds(pl.multiple_of(step * tile, tile), tile)
+
+    def send(src, dst, slot, device):
+        copy = remote(src, dst, send_sem, recv_sem, slot, device)
         copy.start()
-    own.wait()
-    for copy in copies:
-        copy.wait_recv()
-    across = remote(
-        o_ref.at[column], o_ref.at[column], send_sem, recv_sem, owners - 1, sibling
-    )
-    across.start()
-    for copy in copies:
+        sent.append(copy)
+        return copy
+
+    def route(way, values, first):
+        outgoing[way] = (
+            product(placing_ref[...], values)
+            .astype(jnp.bfloat16)
+            .reshape(owners, capacity, width)
+        )
+        if first:
+            meet(peers + [sibling])
+        copies = [
+            send(outgoing.at[way, peer[0]], rows.at[way, column, row], way * 2 * owners + i, peer)
+            for i, peer in enumerate(peers)
+        ]
+        rows[way, column, row] = outgoing[way, row]
+        for copy in copies:
+            copy.wait_recv()
+        return send(
+            rows.at[way, column],
+            rows.at[way, column],
+            way * 2 * owners + owners - 1,
+            sibling,
+        )
+
+    def give_back(way, between, after):
+        base = (way * 2 + 1) * owners
+        across = send(partial.at[way, 1 - column], theirs.at[way], base + owners - 1, sibling)
+        between()
+        across.wait_recv()
+        total[way] = (
+            partial[way, column].astype(jnp.float32) + theirs[way].astype(jnp.float32)
+        ).astype(jnp.bfloat16)
+        copies = [
+            send(total.at[way, peer[0]], arrived.at[way, row], base + i, peer)
+            for i, peer in enumerate(peers)
+        ]
+        arrived[way, row] = total[way, row]
+        after()
+        for copy in copies:
+            copy.wait_recv()
+        return product(placed_ref[...], arrived[way].reshape(count, width))
+
+    def forward(block):
+        values = rows[0, block].reshape(count, width)
+
+        def step(i, summed):
+            pre_act = product(values, w_in_ref[:, part(i)])
+            sigma = jax.nn.sigmoid(pre_act)
+            active = (pre_act * sigma).astype(jnp.bfloat16)
+            hidden[block, :, part(i)] = active
+            slope[block, :, part(i)] = sigma * (1.0 + pre_act * (1.0 - sigma))
+            return summed + product(active, w_out_ref[part(i), :])
+
+        summed = lax.fori_loop(0, units // tile, step, jnp.zeros((count, width), jnp.float32))
+        partial[0, block] = summed.astype(jnp.bfloat16).reshape(owners, capacity, width)
+
+    def backward(block):
+        values = rows[1, block].reshape(count, width)
+
+        def step(i, summed):
+            change = product(values, w_out_ref[part(i), :], contract_cols)
+            change = (change * slope[block, :, part(i)]).astype(jnp.bfloat16)
+            grad_pre[block, :, part(i)] = change
+            return summed + product(change, w_in_ref[:, part(i)], contract_cols)
+
+        summed = lax.fori_loop(0, units // tile, step, jnp.zeros((count, width), jnp.float32))
+        partial[1, block] = summed.astype(jnp.bfloat16).reshape(owners, capacity, width)
+
+    def grads_out():
+        values = rows[1].reshape(2 * count, width)
+
+        def step(i, carry):
+            units_of = hidden[:, :, part(i)].reshape(2 * count, tile)
+            grad_out_ref[part(i), :] = product(units_of, values, contract_rows)
+            return carry
+
+        lax.fori_loop(0, units // tile, step, 0)
+
+    def grads_in():
+        values = rows[0].reshape(2 * count, width)
+
+        def step(i, carry):
+            change = grad_pre[:, :, part(i)].reshape(2 * count, tile)
+            grad_in_ref[:, part(i)] = product(values, change, contract_rows)
+            return carry
+
+        lax.fori_loop(0, units // tile, step, 0)
+
+    def nothing():
+        return None
+
+    across = route(0, normed_ref[...], True)
+    forward(column)
+    across.wait_recv()
+    forward(1 - column)
+    mixture = give_back(0, nothing, nothing)
+    joined = (normed_ref[...].astype(jnp.float32) + mixture).astype(jnp.bfloat16)
+    joined_grad = jnp.zeros(joined.shape, jnp.float32)
+    for k in range(3):
+        tower_pre = product(joined, tow1_ref[k])
+        sigma = jax.nn.sigmoid(tower_pre)
+        gain = tow2_ref[k : k + 1, :]
+        logit = jnp.sum(tower_pre * sigma * gain, axis=-1, keepdims=True)
+        guess = jax.nn.sigmoid(logit) if k < 2 else logit
+        predicted_ref[:, k : k + 1] = guess
+        tower_slope = sigma * (1.0 + tower_pre * (1.0 - sigma))
+        tower_grad = ((guess - targets_ref[:, k : k + 1]) * gain * tower_slope).astype(jnp.bfloat16)
+        joined_grad += product(tower_grad, tow1_ref[k], contract_cols)
+    joined_grad = joined_grad.astype(jnp.bfloat16)
+    across = route(1, joined_grad, False)
+    backward(column)
+    across.wait_recv()
+    backward(1 - column)
+    mixture_grad = give_back(1, grads_out, grads_in)
+    normed_grad_ref[...] = joined_grad.astype(jnp.float32) + mixture_grad
+    for copy in sent:
         copy.wait_send()
-    across.wait()
-
-
-def return_kernel(owners, x_ref, o_ref, theirs, total, send_sem, recv_sem, own_sem):
-    row, column = here()
-    sibling = (row, 1 - column)
-    peers = [(lax.rem(row + step, owners), column) for step in range(1, owners)]
-    meet(peers + [sibling])
-    across = remote(x_ref.at[1 - column], theirs, send_sem, recv_sem, owners - 1, sibling)
-    across.start()
-    across.wait_recv()
-    total[...] = (
-        x_ref[column].astype(jnp.float32) + theirs[...].astype(jnp.float32)
-    ).astype(total.dtype)
-    copies = [
-        remote(total.at[peer[0]], o_ref.at[row], send_sem, recv_sem, i, peer)
-        for i, peer in enumerate(peers)
-    ]
-    for copy in copies:
-        copy.start()
-    own = pltpu.make_async_copy(total.at[row], o_ref.at[row], own_sem)
-    own.start()
-    across.wait_send()
-    own.wait()
-    for copy in copies:
-        copy.wait()
+
+
+def run_experts(normed, placing, weight_in, weight_out, w_tow1, w_tow2, targets, capacity):
+    owners = lax.axis_size("table")
+    width, units = weight_in.shape
+    block = (owners, capacity, width)
+    count = owners * capacity
+    operands = (normed, placing, placing.T, weight_in, weight_out, w_tow1, w_tow2, targets)
+    return pl.pallas_call(
+        experts_kernel,
+        out_shape=[
+            jax.ShapeDtypeStruct(targets.shape, jnp.float32),
+            jax.ShapeDtypeStruct(normed.shape, jnp.float32),
+            jax.ShapeDtypeStruct(weight_in.shape, jnp.float32),
+            jax.ShapeDtypeStruct(weight_out.shape, jnp.float32),
+        ],
+        in_specs=[pl.BlockSpec(memory_space=pltpu.VMEM)] * len(operands),
+        out_specs=[pl.BlockSpec(memory_space=pltpu.VMEM)] * 4,
+        scratch_shapes=[
+            pltpu.VMEM((2,) + block, jnp.bfloat16),
+            pltpu.VMEM((2, 2) + block, jnp.bfloat16),
+            pltpu.VMEM((2, 2) + block, jnp.bfloat16),
+            pltpu.VMEM((2,) + block, jnp.bfloat16),
+            pltpu.VMEM((2,) + block, jnp.bfloat16),
+            pltpu.VMEM((2,) + block, jnp.bfloat16),
+            pltpu.VMEM((2, count, units), jnp.bfloat16),
+            pltpu.VMEM((2, count, units), jnp.float32),
+            pltpu.VMEM((2, count, units), jnp.bfloat16),
+            pltpu.SemaphoreType.DMA((4 * owners,)),
+            pltpu.SemaphoreType.DMA((4 * owners,)),
+        ],
+        compiler_params=pltpu.CompilerParams(
+            collective_id=1, has_side_effects=True, vmem_limit_bytes=40 << 20
+        ),
+    )(*operands)
 
 
 def plane_of(row):
@@ -237,33 +387,15 @@
     return lax.axis_size("expert") == 2 and lax.axis_size("table") == 16
 
 
-def dispatch(buffer, collective_id):
-    if direct():
-        owners = buffer.shape[0]
-        kernel = functools.partial(dispatch_kernel, owners)
-        arrived = call(kernel, buffer, (2,) + buffer.shape, buffer.dtype, (), owners, collective_id)
-        return arrived.reshape(-1, buffer.shape[-1])
+def dispatch(buffer):
     arrived = lax.all_to_all(buffer, "table", split_axis=0, concat_axis=0, tiled=True)
     columns = lax.all_gather(arrived[None], "expert", axis=0, tiled=True)
     return columns.reshape(-1, buffer.shape[-1])
 
 
-def send_back(partial, experts, capacity, collective_id):
+def send_back(partial, experts, capacity):
     width = partial.shape[-1]
     partial = partial.astype(jnp.bfloat16)
-    if direct():
-        block = (experts, capacity, width)
-        kernel = functools.partial(return_kernel, experts)
-        arrived = call(
-            kernel,
-            partial.reshape((2,) + block),
-            block,
-            partial.dtype,
-            (block, block),
-            experts,
-            collective_id,
-        )
-        return arrived.reshape(experts * capacity, width)
     summed = lax.psum_scatter(partial, "expert", scatter_dimension=0, tiled=True)
     arrived = lax.all_to_all(
         summed.reshape(experts, capacity, width), "table", split_axis=0, concat_axis=0, tiled=True
@@ -305,6 +437,57 @@
         arrived = lax.ppermute(theirs, "expert", [(0, 1), (1, 0)])
         return ours.astype(jnp.float32) + arrived.astype(jnp.float32)
     return lax.psum_scatter(row_grad, "expert", scatter_dimension=0, tiled=True).astype(jnp.float32)
+
+
+def route_experts(normed, placing, weight_in, weight_out, w_tow1, w_tow2, targets, capacity):
+    owners = lax.axis_size("table")
+    contract_rows = (((0,), (0,)), ((), ()))
+    contract_cols = (((1,), (1,)), ((), ()))
+    outgoing = jnp.dot(placing, normed, preferred_element_type=jnp.float32).astype(jnp.bfloat16)
+    gathered = dispatch(outgoing.reshape(owners, capacity, outgoing.shape[-1]))
+    pre_act = jnp.dot(gathered, weight_in, preferred_element_type=jnp.float32)
+    hidden = jax.nn.silu(pre_act).astype(jnp.bfloat16)
+
+    forward = jnp.dot(hidden, weight_out, preferred_element_type=jnp.float32)
+    expert_out = send_back(forward, owners, capacity)
+    mixture = lax.dot_general(
+        placing, expert_out, contract_rows, preferred_element_type=jnp.float32
+    )
+    joined = (normed.astype(jnp.float32) + mixture).astype(jnp.bfloat16)
+    tower_pre = jnp.einsum("be,kem->kbm", joined, w_tow1, preferred_element_type=jnp.float32)
+    logits = jnp.sum(jax.nn.silu(tower_pre) * w_tow2[:, None, :], axis=-1)
+    predicted = jnp.stack(
+        [jax.nn.sigmoid(logits[0]), jax.nn.sigmoid(logits[1]), logits[2]], axis=-1
+    )
+    logit_grad = predicted - targets
+    tower_grad = (logit_grad.T[:, :, None] * w_tow2[:, None, :] * silu_slope(tower_pre)).astype(
+        jnp.bfloat16
+    )
+    joined_grad = jnp.einsum(
+        "kbm,kem->be", tower_grad, w_tow1, preferred_element_type=jnp.float32
+    ).astype(jnp.bfloat16)
+    back_rows = jnp.dot(placing, joined_grad, preferred_element_type=jnp.float32).astype(
+        jnp.bfloat16
+    )
+    gathered_grad = dispatch(back_rows.reshape(owners, capacity, back_rows.shape[-1]))
+    grad_hidden = lax.dot_general(
+        gathered_grad, weight_out, contract_cols, preferred_element_type=jnp.float32
+    )
+    grad_pre = (grad_hidden * silu_slope(pre_act)).astype(jnp.bfloat16)
+    grad_out = lax.dot_general(
+        hidden, gathered_grad, contract_rows, preferred_element_type=jnp.float32
+    )
+    grad_in = lax.dot_general(gathered, grad_pre, contract_rows, preferred_element_type=jnp.float32)
+
+    backward = lax.dot_general(
+        grad_pre, weight_in, contract_cols, preferred_element_type=jnp.float32
+    )
+    input_grad = send_back(backward, owners, capacity)
+    mixture_grad = lax.dot_general(
+        placing, input_grad, contract_rows, preferred_element_type=jnp.float32
+    )
+    normed_grad = joined_grad.astype(jnp.float32) + mixture_grad
+    return predicted, normed_grad, grad_in, grad_out
 
 
 def local(
@@ -327,7 +510,6 @@
     capacity = max(2, 2 * samples // owners)
     local_rows = owners * capacity
     contract_rows = (((0,), (0,)), ((), ()))
-    contract_cols = (((1,), (1,)), ((), ()))
     window = windows[0, 0]
     row_select = (
         jnp.arange(table.shape[1], dtype=jnp.int32)[:, None] == window[None, :]
@@ -353,52 +535,10 @@
     placing = (jnp.arange(local_rows, dtype=jnp.int32)[:, None] == target_slot[None, :]).astype(
         jnp.bfloat16
     )
-    outgoing = jnp.dot(placing, normed, preferred_element_type=jnp.float32).astype(jnp.bfloat16)
-    gathered = dispatch(outgoing.reshape(owners, capacity, outgoing.shape[-1]), 1)
-    weight_in = w_in[0]
-    weight_out = w_out[0]
-    pre_act = jnp.dot(gathered, weight_in, preferred_element_type=jnp.float32)
-    hidden = jax.nn.silu(pre_act).astype(jnp.bfloat16)
-
-    forward = jnp.dot(hidden, weight_out, preferred_element_type=jnp.float32)
-    expert_out = send_back(forward, owners, capacity, 2)
-    mixture = lax.dot_general(
-        placing, expert_out, contract_rows, preferred_element_type=jnp.float32
-    )
-    joined = (normed.astype(jnp.float32) + mixture).astype(jnp.bfloat16)
-    tower_pre = jnp.einsum("be,kem->kbm", joined, w_tow1, preferred_element_type=jnp.float32)
-    logits = jnp.sum(jax.nn.silu(tower_pre) * w_tow2[:, None, :], axis=-1)
-    predicted = jnp.stack(
-        [jax.nn.sigmoid(logits[0]), jax.nn.sigmoid(logits[1]), logits[2]], axis=-1
-    )
-    logit_grad = predicted - targets[0]
-    tower_grad = (logit_grad.T[:, :, None] * w_tow2[:, None, :] * silu_slope(tower_pre)).astype(
-        jnp.bfloat16
-    )
-    joined_grad = jnp.einsum(
-        "kbm,kem->be", tower_grad, w_tow1, preferred_element_type=jnp.float32
-    ).astype(jnp.bfloat16)
-    back_rows = jnp.dot(placing, joined_grad, preferred_element_type=jnp.float32).astype(
-        jnp.bfloat16
-    )
-    gathered_grad = dispatch(back_rows.reshape(owners, capacity, back_rows.shape[-1]), 3)
-    grad_hidden = lax.dot_general(
-        gathered_grad, weight_out, contract_cols, preferred_element_type=jnp.float32
-    )
-    grad_pre = (grad_hidden * silu_slope(pre_act)).astype(jnp.bfloat16)
-    grad_out = lax.dot_general(
-        hidden, gathered_grad, contract_rows, preferred_element_type=jnp.float32
-    )
-    grad_in = lax.dot_general(gathered, grad_pre, contract_rows, preferred_element_type=jnp.float32)
-
-    backward = lax.dot_general(
-        grad_pre, weight_in, contract_cols, preferred_element_type=jnp.float32
-    )
-    input_grad = send_back(backward, owners, capacity, 4)
-    mixture_grad = lax.dot_general(
-        placing, input_grad, contract_rows, preferred_element_type=jnp.float32
-    )
-    normed_grad = joined_grad.astype(jnp.float32) + mixture_grad
+    run = run_experts if direct() else route_experts
+    predicted, normed_grad, grad_in, grad_out = run(
+        normed, placing, w_in[0], w_out[0], w_tow1, w_tow2, targets[0], capacity
+    )
     scaled_grad = normed_grad * norm_gain
     summed_grad = inverse * (
         scaled_grad

time: 107 us -> 97.2 us (0.908)
  matrix products: 23.8 us -> 5.72 us
  local copies, waits for them, and re-layouts: 2.45 us -> 10.7 us
  Pallas kernels: 75.1 us -> 71.5 us
  other arithmetic: 4.62 us -> 7.14 us
    pallas_call x6 -> x2, Pallas kernels: 75.1 us -> 35.2 us  [call(): pl.pallas_call(kernel, out_shape=jax.ShapeDtypeStruct(shape, dtype), in_s...]
    pallas_call x0 -> x1, Pallas kernels: none -> 36.3 us  [run_experts(): pl.pallas_call(experts_kernel, out_shape=[jax.ShapeDtypeStruct(targets.sh...]
    dot_general x11 -> x0, matrix products: 19.1 us -> none  [the longest x1 3.91 us: local(): lax.dot_general(gathered_grad, weight_out, contract_cols, preferred_eleme...]
    unnamed x23 -> x28, local copies, waits for them, and re-layouts: 1.68 us -> 9.76 us
  transfers between devices with their start and end apart: 1 -> 1, of which waited for: 0 -> 1; matrix products, arithmetic and copies ran while one was open for 7% -> 1% of each run, Pallas kernels for 0% -> 0%
where the time goes in v3:
time: 97.2 us; the launch traced here: 96.7 us
  Pallas kernels  71.5 us (74%)
  local copies, waits for them, and re-layouts  10.7 us (11%)
  other arithmetic  7.14 us (7%)
  matrix products  5.72 us (6%)
    pallas_call x1, Pallas kernels, run_experts(): pl.pallas_call(experts_kernel, out_shape=[jax.ShapeDtypeStruct(targets.sh...  36.3 us
    pallas_call x2, Pallas kernels, call(): pl.pallas_call(kernel, out_shape=jax.ShapeDtypeStruct(shape, dtype), in_s...  35.2 us
    unnamed x28, local copies, waits for them, and re-layouts  9.76 us
    dot_general x1, matrix products, local(): jnp.dot(row_select, window_grad.astype(jnp.bfloat16), preferred_element_t...  2.67 us
    dot_general x1, matrix products, local(): lax.dot_general(counts, dequant, contract_rows, preferred_element_type=jn...  2.16 us
    reduce_sum x1, other arithmetic, bag_counts(): return jnp.sum(hits, axis=0).astype(jnp.bfloat16)  2.11 us
  transfers between devices with their start and end apart: 1, of which 1 were waited for; matrix products, arithmetic and copies ran while one was open for 1% of the time, Pallas kernels for 0%

profile of v3, /device:TPU:0, one launch (start us, length us, event | category | flops | bytes accessed | tf_op | source)
XLA Modules:
  0.0 96.7 jit_solution(14842822777321059837)
XLA Ops:
  0.6 0.0 copy-start
  0.6 0.9 fusion.4
  1.5 0.7 convert_add_fusion
  2.2 0.1 fusion.23.placed_ref
  2.3 0.9 bitcast_select_fusion
  3.2 2.1 %convert_reduce_fusion = bf16[256,2048]{1,0:T(8,128)(2,1)S(1)} fusion(s32[8,2048]{1,0:T(8,128)S(1)} %bitcast_select_fusion), kind=kLoop, calls=%fused_computation | loop fusion | flops 12058624 | bytes 1114112 | tf_op jit(solution)/shard_map/reduce_sum | solution.py:23
  5.3 0.0 copy-start.6
  5.3 0.0 copy-done
  5.3 0.0 copy-start.11
  5.4 0.0 copy-start.10
  5.4 0.0 copy-start.7
  5.4 0.0 copy-start.2
  5.4 2.2 %fusion.2 = bf16[2048,256]{1,0:T(8,128)(2,1)S(1)} fusion(f32[256]{0:T(256)S(1)} %bitcast.39, bf16[256,2048]{1,0:T(8,128)(2,1)S(1)} %convert_reduce_fusion, bf16[1,512,256]{2,1,0:T(8,128)(2,1)} %param.13, f32[512]{0:T(512)} %bitcast.41, s32[256]{0:T(256)} %bitcast.42), kind=kOutput, calls=%fused_computation.5 | convolution fusion | flops 338362368 | bytes 2363392 | tf_op jit(solution)/shard_map/dot_general | solution.py:522
  7.6 18.7 %shard_map.156 = f32[128,256]{1,0:T(8,128)S(1)} custom-call(bf16[16,128,256]{2,1,0:T(8,128)(2,1)S(1)} %bitcast.32), custom_call_target="tpu_custom_call" | custom-call | tf_op jit(solution)/shard_map/pallas_call | solution.py:373
  26.2 0.0 copy-done.6
  26.2 0.0 copy-done.11
  26.2 0.1 multiply_reduce_fusion.1
  26.4 0.0 copy-done.10
  26.4 0.0 copy-start.8
  26.4 0.1 copy.19
  26.5 0.0 copy-done.7
  26.5 0.1 multiply_convert_fusion.1.normed_ref
  26.6 0.3 copy-done.8
  26.9 0.0 copy-done.2
  26.9 0.0 copy-start.3
  26.9 1.2 %copy-done.3 = bf16[1,2048,256]{2,1,0:T(8,128)(2,1)S(1)} copy-done((bf16[1,2048,256]{2,1,0:T(8,128)(2,1)S(1)}, bf16[1,2048,256]{2,1,0:T(8,128)(2,1)}, u32[]{:S(2)}) %copy-start.3) | copy-done | bytes 1048600
  28.1 0.0 copy-start.4
  28.1 1.0 %copy-done.4 = bf16[3,256,256]{2,1,0:T(8,128)(2,1)S(1)} copy-done((bf16[3,256,256]{2,1,0:T(8,128)(2,1)S(1)}, bf16[3,256,256]{2,1,0:T(8,128)(2,1)}, u32[]{:S(2)}) %copy-start.4) | copy-done | bytes 393240
  29.1 0.0 copy-start.5
  29.1 0.7 copy-done.5
  29.8 0.0 copy-start.9
  29.8 36.3 %shard_map.157 = (f32[128,3]{1,0:T(8,128)S(1)}, f32[128,256]{1,0:T(8,128)S(1)}, f32[256,2048]{1,0:T(8,128)S(1)}, f32[2048,256]{1,0:T(8,128)S(1)}) custom-call(bf16[128,256]{1,0:T(8,128)(2,1)S(1)} %multiply_convert_fusion.1.normed_ref, bf16[256,128]{1,0:T(8,128)(2,1)S(1)} %fusion.22.placing_ref, bf16[128,256]{1,0:T(8,128)(2,1)S(1)} %fusion.23.placed_ref, ...), custom_call_target="tpu_custom_call" | custom-call | tf_op jit(solution)/shard_map/pallas_call | solution.py:219
  66.1 0.0 copy-start.1
  66.2 1.3 %copy-done.1 = f32[256,2048]{1,0:T(8,128)} copy-done((f32[256,2048]{1,0:T(8,128)}, f32[256,2048]{1,0:T(8,128)S(1)}, u32[]{:S(2)}) %copy-start.1) | copy-done | bytes 2097176
  67.5 0.8 multiply_reduce_fusion
  68.3 0.0 copy-done.9
  68.3 0.8 multiply_convert_fusion.x_ref
  69.1 16.6 %shard_map.158 = bf16[16,128,256]{2,1,0:T(8,128)(2,1)S(1)} custom-call(bf16[128,256]{1,0:T(8,128)(2,1)S(1)} %multiply_convert_fusion.x_ref), custom_call_target="tpu_custom_call" | custom-call | tf_op jit(solution)/shard_map/pallas_call | solution.py:373
  85.6 2.7 %convolution_convert_fusion.1 = bf16[512,256]{1,0:T(8,128)(2,1)} fusion(bf16[2048,256]{1,0:T(8,128)(2,1)S(1)} %bitcast.35, bf16[256,2048]{1,0:T(8,128)(2,1)} %copy-done.6, s32[256]{0:T(256)} %bitcast.43, f32[256]{0:T(256)} %bitcast.40), kind=kOutput, calls=%fused_computation.6 | convolution fusion | flops 335937536 | bytes 2361344 | tf_op jit(solution)/shard_map/dot_general | solution.py:549
  88.3 0.9 constant_dynamic-slice_fusion
  89.2 0.1 collective-permute-start
  89.3 0.6 copy.20
  89.9 0.7 collective-permute-done
  90.6 1.6 %add_bitcast_fusion = f32[1,256,256]{2,1,0:T(8,128)} fusion(bf16[256,256]{1,0:T(8,128)(2,1)S(1)} %collective-permute-done, bf16[512,256]{1,0:T(8,128)(2,1)} %convolution_convert_fusion.1, s32[]{:T(128)S(6)} %select_n.15), kind=kLoop, calls=%fused_computation.19 | loop fusion | flops 196608 | bytes 524292 | tf_op jit(solution)/shard_map/broadcast_in_dim | solution.py:553
  92.3 3.1 %copy.23 = f32[1,256,2048]{2,1,0:T(8,128)} copy(f32[1,256,2048]{2,1,0:T(8,128)} %bitcast.31) | data formatting | bytes 4194304
  95.4 1.3 %copy.24 = f32[1,2048,256]{2,1,0:T(8,128)} copy(f32[1,2048,256]{2,1,0:T(8,128)S(1)} %bitcast.30) | data formatting | bytes 4194304
  (4 shorter events, 0.0 us)
Async XLA Ops:
  0.6 4.7 %copy-start = (f32[16,256]{1,0:T(8,128)S(1)}, f32[16,256]{1,0:T(8,128)}, u32[]{:S(2)}) copy-start(f32[16,256]{1,0:T(8,128)} %param.18) | copy-start | bytes 49156
  5.3 20.9 %copy-start.6 = (bf16[256,2048]{1,0:T(8,128)(2,1)}, bf16[256,2048]{1,0:T(8,128)(2,1)S(1)}, u32[]{:S(2)}) copy-start(bf16[256,2048]{1,0:T(8,128)(2,1)S(1)} %convert_reduce_fusion) | copy-start | bytes 3145732
  5.3 20.9 %copy-start.11 = (f32[1,256]{1,0:T(1,128)}, f32[1,256]{1,0:T(1,128)S(1)}, u32[]{:S(2)}) copy-start(f32[1,256]{1,0:T(1,128)S(1)} %constant_dynamic-slice_fusion.1) | copy-start | bytes 3076
  5.4 21.0 %copy-start.10 = (f32[1,128,3]{1,0,2:T(1,128)S(1)}, f32[1,128,3]{1,0,2:T(1,128)}, u32[]{:S(2)}) copy-start(f32[1,128,3]{1,0,2:T(1,128)} %param.25) | copy-start | bytes 4612
  5.4 21.1 %copy-start.7 = (f32[256]{0:T(256)S(1)}, f32[256]{0:T(256)}, u32[]{:S(2)}) copy-start(f32[256]{0:T(256)} %param.19) | copy-start | bytes 3076
  5.4 21.5 %copy-start.2 = (bf16[1,256,2048]{2,1,0:T(8,128)(2,1)S(1)}, bf16[1,256,2048]{2,1,0:T(8,128)(2,1)}, u32[]{:S(2)}) copy-start(bf16[1,256,2048]{2,1,0:T(8,128)(2,1)} %param.21) | copy-start | bytes 3145732
  26.4 0.5 copy-start.8
  26.9 1.2 %copy-start.3 = (bf16[1,2048,256]{2,1,0:T(8,128)(2,1)S(1)}, bf16[1,2048,256]{2,1,0:T(8,128)(2,1)}, u32[]{:S(2)}) copy-start(bf16[1,2048,256]{2,1,0:T(8,128)(2,1)} %param.22) | copy-start | bytes 3145732
  28.1 1.0 %copy-start.4 = (bf16[3,256,256]{2,1,0:T(8,128)(2,1)S(1)}, bf16[3,256,256]{2,1,0:T(8,128)(2,1)}, u32[]{:S(2)}) copy-start(bf16[3,256,256]{2,1,0:T(8,128)(2,1)} %tow1_ref.1) | copy-start | bytes 1179652
  29.1 0.7 copy-start.5
  29.8 38.5 %copy-start.9 = (f32[128]{0:T(128)S(1)}, f32[128]{0:T(128)}, u32[]{:S(2)}) copy-start(f32[128]{0:T(128)} %copy-done.8) | copy-start | bytes 1540
  66.1 1.3 %copy-start.1 = (f32[256,2048]{1,0:T(8,128)}, f32[256,2048]{1,0:T(8,128)S(1)}, u32[]{:S(2)}) copy-start(f32[256,2048]{1,0:T(8,128)S(1)} %get-tuple-element.10) | copy-start | bytes 6291460
  89.2 1.4 %collective-permute-start = (bf16[256,256]{1,0:T(8,128)(2,1)S(1)}, bf16[256,256]{1,0:T(8,128)(2,1)S(1)}, u32[]{:S(2)}, u32[]{:S(2)}) collective-permute-start(bf16[256,256]{1,0:T(8,128)(2,1)S(1)} %constant_dynamic-slice_fusion), channel_id=1, source_target_pairs={{0,1},{1,0},{2,3},{3,2},{4,5},{5,4},{6,7},{7,6},{8,9},{9,8},{10,11... | collective-permute-start | bytes 393224 | tf_op jit(solution)/shard_map/ppermute | solution.py:437

commit v4 on v3

--- a/solution.py
+++ b/solution.py
@@ -49,9 +49,9 @@
     normed_ref,
     placing_ref,
     placed_ref,
-    w_in_ref,
-    w_out_ref,
-    tow1_ref,
+    w_in_far,
+    w_out_far,
+    tow1_far,
     tow2_ref,
     targets_ref,
     predicted_ref,
@@ -67,8 +67,12 @@
     hidden,
     slope,
     grad_pre,
+    w_in_ref,
+    w_out_ref,
+    tow1_ref,
     send_sem,
     recv_sem,
+    load_sem,
 ):
     owners, capacity, width = outgoing.shape[1:]
     count = owners * capacity
@@ -182,7 +186,17 @@
     def nothing():
         return None
 
+    loads = [
+        pltpu.make_async_copy(far, near, load_sem.at[i])
+        for i, (far, near) in enumerate(
+            ((w_in_far, w_in_ref), (w_out_far, w_out_ref), (tow1_far, tow1_ref))
+        )
+    ]
+    for load in loads:
+        load.start()
     across = route(0, normed_ref[...], True)
+    for load in loads:
+        load.wait()
     forward(column)
     across.wait_recv()
     forward(1 - column)
@@ -224,7 +238,10 @@
             jax.ShapeDtypeStruct(weight_in.shape, jnp.float32),
             jax.ShapeDtypeStruct(weight_out.shape, jnp.float32),
         ],
-        in_specs=[pl.BlockSpec(memory_space=pltpu.VMEM)] * len(operands),
+        in_specs=[
+            pl.BlockSpec(memory_space=pl.ANY if i in (3, 4, 5) else pltpu.VMEM)
+            for i in range(len(operands))
+        ],
         out_specs=[pl.BlockSpec(memory_space=pltpu.VMEM)] * 4,
         scratch_shapes=[
             pltpu.VMEM((2,) + block, jnp.bfloat16),
@@ -236,11 +253,15 @@
             pltpu.VMEM((2, count, units), jnp.bfloat16),
             pltpu.VMEM((2, count, units), jnp.float32),
             pltpu.VMEM((2, count, units), jnp.bfloat16),
+            pltpu.VMEM(weight_in.shape, weight_in.dtype),
+            pltpu.VMEM(weight_out.shape, weight_out.dtype),
+            pltpu.VMEM(w_tow1.shape, w_tow1.dtype),
             pltpu.SemaphoreType.DMA((4 * owners,)),
             pltpu.SemaphoreType.DMA((4 * owners,)),
+            pltpu.SemaphoreType.DMA((3,)),
         ],
         compiler_params=pltpu.CompilerParams(
-            collective_id=1, has_side_effects=True, vmem_limit_bytes=40 << 20
+            collective_id=1, has_side_effects=True, vmem_limit_bytes=60 << 20
         ),
     )(*operands)
 
@@ -378,7 +399,7 @@
         scratch_shapes=[pltpu.VMEM(s, jnp.bfloat16) for s in scratch] + semaphores
         + ([] if kernel is scatter_kernel else [pltpu.SemaphoreType.DMA]),
         compiler_params=pltpu.CompilerParams(
-            collective_id=collective_id, has_side_effects=True, vmem_limit_bytes=32 << 20
+            collective_id=collective_id, has_side_effects=True, vmem_limit_bytes=8 << 20
         ),
     )(operand)
 

time: 97.2 us -> 95.2 us (0.979)
  local copies, waits for them, and re-layouts: 10.7 us -> 5.1 us
  Pallas kernels: 71.5 us -> 74.5 us
  other arithmetic: 7.14 us -> 8.6 us
    unnamed x28 -> x20, local copies, waits for them, and re-layouts: 9.76 us -> 5.08 us
    pallas_call x1, Pallas kernels: 36.3 us -> 39.3 us  [run_experts(): pl.pallas_call(experts_kernel, out_shape=[jax.ShapeDtypeStruct(targets.sh...]
    convert_element_type x2, other arithmetic: 0.11 us -> 1.35 us  [local(): (jnp.arange(local_rows, dtype=jnp.int32)[:, None] == target_slot[None, :]...]
where the time goes in v4:
time: 95.2 us; the launch traced here: 94.8 us
  Pallas kernels  74.5 us (78%)
  other arithmetic  8.6 us (9%)
  local copies, waits for them, and re-layouts  5.1 us (5%)
  matrix products  4.96 us (5%)
    pallas_call x1, Pallas kernels, run_experts(): pl.pallas_call(experts_kernel, out_shape=[jax.ShapeDtypeStruct(targets.sh...  39.3 us
    pallas_call x2, Pallas kernels, call(): pl.pallas_call(kernel, out_shape=jax.ShapeDtypeStruct(shape, dtype), in_s...  35.2 us
    unnamed x20, local copies, waits for them, and re-layouts  5.08 us
    reduce_sum x1, other arithmetic, bag_counts(): return jnp.sum(hits, axis=0).astype(jnp.bfloat16)  2.11 us
    dot_general x1, matrix products, local(): lax.dot_general(counts, dequant, contract_rows, preferred_element_type=jn...  2.1 us
    dot_general x1, matrix products, local(): jnp.dot(row_select, window_grad.astype(jnp.bfloat16), preferred_element_t...  1.98 us
  transfers between devices with their start and end apart: 1, of which 1 were waited for; matrix products, arithmetic and copies ran while one was open for 1% of the time, Pallas kernels for 0%

profile of v4, /device:TPU:0, one launch (start us, length us, event | category | flops | bytes accessed | tf_op | source)
XLA Modules:
  0.0 94.8 jit_solution(9044902823713848341)
XLA Ops:
  0.6 0.0 copy-start
  0.6 0.9 fusion.4
  1.5 0.7 convert_add_fusion
  2.2 0.7 fusion.22.placing_ref
  2.9 0.7 fusion.23.placed_ref
  3.6 0.9 bitcast_select_fusion
  4.4 2.1 %convert_reduce_fusion = bf16[256,2048]{1,0:T(8,128)(2,1)S(1)} fusion(s32[8,2048]{1,0:T(8,128)S(1)} %bitcast_select_fusion), kind=kLoop, calls=%fused_computation | loop fusion | flops 12058624 | bytes 1114112 | tf_op jit(solution)/shard_map/reduce_sum | solution.py:23
  6.5 0.0 copy-start.3
  6.5 0.0 copy-done
  6.6 0.0 copy-start.6
  6.6 0.0 copy-start.5
  6.6 2.1 %fusion.2 = bf16[2048,256]{1,0:T(8,128)(2,1)S(1)} fusion(f32[256]{0:T(256)S(1)} %bitcast.39, bf16[256,2048]{1,0:T(8,128)(2,1)S(1)} %convert_reduce_fusion, bf16[1,512,256]{2,1,0:T(8,128)(2,1)} %param.13, f32[512]{0:T(512)} %bitcast.41, s32[256]{0:T(256)} %bitcast.42), kind=kOutput, calls=%fused_computation.5 | convolution fusion | flops 338362368 | bytes 2363392 | tf_op jit(solution)/shard_map/dot_general | solution.py:543
  8.7 18.7 %shard_map.156 = f32[128,256]{1,0:T(8,128)S(1)} custom-call(bf16[16,128,256]{2,1,0:T(8,128)(2,1)S(1)} %bitcast.30), custom_call_target="tpu_custom_call" | custom-call | tf_op jit(solution)/shard_map/pallas_call | solution.py:394
  27.4 0.0 copy-done.3
  27.4 0.1 multiply_reduce_fusion.1
  27.5 0.0 copy-done.6
  27.5 0.7 copy.19
  28.2 0.0 copy-done.5
  28.2 0.7 multiply_convert_fusion.1.normed_ref
  29.0 0.0 copy-start.7
  29.0 39.3 %shard_map.157 = (f32[128,3]{1,0:T(8,128)}, f32[128,256]{1,0:T(8,128)}, f32[256,2048]{1,0:T(8,128)}, f32[2048,256]{1,0:T(8,128)}) custom-call(bf16[128,256]{1,0:T(8,128)(2,1)} %multiply_convert_fusion.1.normed_ref, bf16[256,128]{1,0:T(8,128)(2,1)} %fusion.22.placing_ref, bf16[128,256]{1,0:T(8,128)(2,1)} %fusion.23.placed_ref, bf16[256,2048]{1,0:T(8,128)(2,1)} %bitcast.34, ...), custom_call_target="tpu_custom_call" | custom-call | tf_op jit(solution)/shard_map/pallas_call | solution.py:233
  68.2 1.0 %multiply_reduce_fusion = f32[128]{0:T(128)S(1)} fusion(f32[128,256]{1,0:T(8,128)S(1)} %shard_map.156, f32[128,256]{1,0:T(8,128)} %get-tuple-element.9, f32[256]{0:T(256)S(1)} %copy-done.5), kind=kLoop, calls=%fused_computation.26 | loop fusion | flops 98176 | bytes 263680 | tf_op jit(solution)/shard_map/reduce_sum | solution.py:566
  69.3 0.0 copy-start.4
  69.3 1.0 %multiply_convert_fusion.x_ref = bf16[128,256]{1,0:T(8,128)(2,1)S(1)} fusion(f32[128,256]{1,0:T(8,128)} %get-tuple-element.9, f32[128,256]{1,0:T(8,128)S(1)} %shard_map.156, f32[128]{0:T(128)S(1)} %broadcast_multiply_fusion, f32[256]{0:T(256)S(1)} %copy-done.5, f32[128]{0:T(128)S(1)} %add_rsqrt_fusion), kind=kLoop, calls=%fused_computation.25 | loop fusion | flops 229376 | bytes 329728 | tf_op jit(solution)/shard_map/convert_element_type | solution.py:568
  70.3 0.0 copy-start.2
  70.3 16.6 %shard_map.158 = bf16[16,128,256]{2,1,0:T(8,128)(2,1)S(1)} custom-call(bf16[128,256]{1,0:T(8,128)(2,1)S(1)} %multiply_convert_fusion.x_ref), custom_call_target="tpu_custom_call" | custom-call | tf_op jit(solution)/shard_map/pallas_call | solution.py:394
  86.9 0.0 copy-done.7
  86.9 2.0 %convolution_convert_fusion.1 = bf16[512,256]{1,0:T(8,128)(2,1)S(1)} fusion(bf16[2048,256]{1,0:T(8,128)(2,1)S(1)} %bitcast.31, bf16[256,2048]{1,0:T(8,128)(2,1)} %copy-done.3, s32[256]{0:T(256)S(1)} %bitcast.43, f32[256]{0:T(256)S(1)} %bitcast.40), kind=kOutput, calls=%fused_computation.6 | convolution fusion | flops 335937536 | bytes 2361344 | tf_op jit(solution)/shard_map/dot_general | solution.py:570
  88.9 0.1 collective-permute-start
  89.0 0.0 copy-done.4
  89.0 0.6 copy.20
  89.7 0.7 collective-permute-done
  90.4 0.7 add_bitcast_fusion
  91.1 0.0 copy-done.2
  91.1 0.0 copy-start.1
  91.1 1.3 %copy.23 = f32[1,256,2048]{2,1,0:T(8,128)} copy(f32[1,256,2048]{2,1,0:T(8,128)S(1)} %bitcast.33) | data formatting | bytes 4194304
  92.4 1.0 %copy-done.1 = f32[2048,256]{1,0:T(8,128)S(1)} copy-done((f32[2048,256]{1,0:T(8,128)S(1)}, f32[2048,256]{1,0:T(8,128)}, u32[]{:S(2)}) %copy-start.1) | copy-done | bytes 2097176
  93.4 1.3 %copy.24 = f32[1,2048,256]{2,1,0:T(8,128)} copy(f32[1,2048,256]{2,1,0:T(8,128)S(1)} %bitcast.32) | data formatting | bytes 4194304
  (4 shorter events, 0.0 us)
Async XLA Ops:
  0.6 5.9 %copy-start = (f32[16,256]{1,0:T(8,128)S(1)}, f32[16,256]{1,0:T(8,128)}, u32[]{:S(2)}) copy-start(f32[16,256]{1,0:T(8,128)} %param.18) | copy-start | bytes 49156
  6.5 20.8 %copy-start.3 = (bf16[256,2048]{1,0:T(8,128)(2,1)}, bf16[256,2048]{1,0:T(8,128)(2,1)S(1)}, u32[]{:S(2)}) copy-start(bf16[256,2048]{1,0:T(8,128)(2,1)S(1)} %convert_reduce_fusion) | copy-start | bytes 3145732
  6.6 20.9 %copy-start.6 = (f32[1,128,3]{1,0,2:T(1,128)S(1)}, f32[1,128,3]{1,0,2:T(1,128)}, u32[]{:S(2)}) copy-start(f32[1,128,3]{1,0,2:T(1,128)} %param.25) | copy-start | bytes 4612
  6.6 21.7 %copy-start.5 = (f32[256]{0:T(256)S(1)}, f32[256]{0:T(256)}, u32[]{:S(2)}) copy-start(f32[256]{0:T(256)} %param.19) | copy-start | bytes 3076
  29.0 58.0 %copy-start.7 = (s32[1,1,256]{2,1,0:T(1,128)S(1)}, s32[1,1,256]{2,1,0:T(1,128)}, u32[]{:S(2)}) copy-start(s32[1,1,256]{2,1,0:T(1,128)} %param.15) | copy-start | bytes 3076
  69.3 19.8 %copy-start.4 = (f32[128,3]{1,0:T(8,128)S(1)}, f32[128,3]{1,0:T(8,128)}, u32[]{:S(2)}) copy-start(f32[128,3]{1,0:T(8,128)} %get-tuple-element.8) | copy-start | bytes 4612
  70.3 20.8 %copy-start.2 = (f32[256,2048]{1,0:T(8,128)S(1)}, f32[256,2048]{1,0:T(8,128)}, u32[]{:S(2)}) copy-start(f32[256,2048]{1,0:T(8,128)} %get-tuple-element.10) | copy-start | bytes 6291460
  88.9 1.4 %collective-permute-start = (bf16[256,256]{1,0:T(8,128)(2,1)S(1)}, bf16[256,256]{1,0:T(8,128)(2,1)S(1)}, u32[]{:S(2)}, u32[]{:S(2)}) collective-permute-start(bf16[256,256]{1,0:T(8,128)(2,1)S(1)} %constant_dynamic-slice_fusion), channel_id=1, source_target_pairs={{0,1},{1,0},{2,3},{3,2},{4,5},{5,4},{6,7},{7,6},{8,9},{9,8},{10,11... | collective-permute-start | bytes 393224 | tf_op jit(solution)/shard_map/ppermute | solution.py:458
  91.1 2.3 %copy-start.1 = (f32[2048,256]{1,0:T(8,128)S(1)}, f32[2048,256]{1,0:T(8,128)}, u32[]{:S(2)}) copy-start(f32[2048,256]{1,0:T(8,128)} %get-tuple-element.11) | copy-start | bytes 6291460
